TPU v7x, 1024 devices: a whole 4x4x32 slice. The times are simulated.
1024 devices in a mesh: gx: 8 (over y, core), gy: 32 (over z), gz: 4 (over x).
Axes of the slice: x: 4, y: 4, z: 32, core: 2. Of those that a mesh axis runs over, the one named last changes fastest.
Arguments:
- u_wind: float32 [64, 256, 3072], P('gz', 'gx', 'gy'), may hold values from -6 to 6
- theta: float32 [64, 256, 3072], P('gz', 'gx', 'gy'), may hold values from -6 to 6
- act_points: float32 [4, 8, 32, 1024], P(None, 'gx', 'gy'), may hold values from -8 to 3072, as said below
- point_count: int32 [8, 32], P('gx', 'gy'), may hold values from 1 to 1024, as said below
- klass: int32 [256, 3072], P('gx', 'gy'), may hold values from 0 to 15
- diff_table: float32 [16, 64], replicated, may hold values from 30 to 3000
Outputs:
- u_next: float32 [64, 256, 3072], P('gz', 'gx', 'gy')
- theta_next: float32 [64, 256, 3072], P('gz', 'gx', 'gy')
Inputs may be any that keep to these rules, and one draw needn't show every extreme that they name: `act_points`: coordinates of the points of tile (p, q) lie in [p * 32, (p+1) * 32), [q * 96, (q+1) * 96) and [0, 64); the force component lies in [-8, 8]. Only the first point_count[p, q] slots of tile (p, q) are live; the force entries of the other slots are arbitrary values that the weight step masks out. In every draw some tile has all 1024 slots live.
All inputs are finite; a program needn't handle non-finite values.
Results may differ from a plain program's by a relative error of at most 0.0003.
Values sent between devices are 32-bit elements; how exact they have to be, the bound alone decides.
No kernel may reach another device: no remote copies, remote signals or barrier semaphores. Data moves between devices by JAX's collectives and lax.ppermute only.
A program may use at most 32 MiB of HBM per device.

v0:
```python
import jax
import jax.numpy as jnp
from jax import lax
from jax.sharding import PartitionSpec as P

HALO = 16


HIGH = lax.Precision.HIGHEST
THETA_SCALE = 1.25
block_depth = 4


def padded_2(x, sides, width):
    for axis, dim in sides:
        peers, length = (lax.axis_size(axis), x.shape[dim])
        up = [(i, (i + 1) % peers) for i in range(peers - 1)]
        down = [(j, i) for i, j in up]
        last = lax.slice_in_dim(x, length - width, length, axis=dim)
        first = lax.slice_in_dim(x, 0, width, axis=dim)
        before = lax.ppermute(last, axis, up)
        after = lax.ppermute(first, axis, down)
        x = jnp.concatenate([before, x, after], axis=dim)
    return x


def kernel_table(coords, centres, smear):
    offset = (coords[:, None] - centres[None, :]) / smear
    return jnp.exp(-offset * offset)


def fold_edges(padded, dim, inner, margin):
    middle = lax.slice_in_dim(padded, 2 * margin, 2 * margin + inner, axis=dim)
    first = lax.slice_in_dim(padded, 0, margin, axis=dim)
    last = lax.slice_in_dim(padded, inner + 3 * margin, inner + 4 * margin, axis=dim)
    pads_first = [(0, 0)] * padded.ndim
    pads_last = [(0, 0)] * padded.ndim
    pads_first[dim] = (0, inner - margin)
    pads_last[dim] = (inner - margin, 0)
    return middle + jnp.pad(first, pads_first) + jnp.pad(last, pads_last)


def fold_columns(padded, inner, margin):
    extent = inner + 4 * margin
    source = lax.broadcasted_iota(jnp.int32, (extent, inner), 0)
    target = lax.broadcasted_iota(jnp.int32, (extent, inner), 1)
    centre_hit = source - 2 * margin == target
    first_hit = (source < margin) & (source == target)
    last_hit = (source >= inner + 3 * margin) & (source - 4 * margin == target)
    folding = (centre_hit | first_hit | last_hit).astype(jnp.float32)
    return jnp.dot(padded, folding, precision=HIGH)


def tridiagonal(lower, diag, upper, rhs):

    def forward(carry, row):
        prev_mod, prev_right = carry
        low_c, mid_c, up_c, right = row
        denom = mid_c - low_c * prev_mod
        next_mod = up_c / denom
        next_right = (right - low_c * prev_right) / denom
        return ((next_mod, next_right), (next_mod, next_right))

    start = (jnp.zeros_like(diag[0]), jnp.zeros_like(rhs[0]))
    _, (mods, rights) = lax.scan(forward, start, (lower, diag, upper, rhs))

    def backward(later, row):
        mod_c, right = row
        value = right - mod_c * later
        return (value, value)

    _, values = lax.scan(backward, jnp.zeros_like(rhs[0]), (mods, rights), reverse=True)
    return values


def shards(u_wind, theta, act_points, point_count, klass, diff_table):
    levels_dev, rows_dev, cols_dev = u_wind.shape
    count_slots = act_points.shape[3]
    smear = HALO / 2.0
    tile_x = lax.axis_index("gx")
    tile_y = lax.axis_index("gy")
    slab = lax.axis_index("gz")
    points = act_points[:, 0, 0, :]
    weight = points[3] * (jnp.arange(count_slots) < point_count[0, 0]).astype(jnp.float32)
    along_x = (tile_x * rows_dev - HALO + jnp.arange(rows_dev + 2 * HALO)).astype(jnp.float32)
    along_y = (tile_y * cols_dev - HALO + jnp.arange(cols_dev + 2 * HALO)).astype(jnp.float32)
    global_level = slab * levels_dev + jnp.arange(levels_dev)
    kern_x = kernel_table(along_x, points[0], smear)
    kern_y = kernel_table(along_y, points[1], smear).T * weight[:, None]
    kern_z = kernel_table(global_level.astype(jnp.float32), points[2], smear)
    kern_z = kern_z.reshape(levels_dev // block_depth, block_depth, count_slots)

    def block_force(kern_part):
        left = (kern_part[:, None, :] * kern_x[None, :, :]).reshape(
            block_depth * kern_x.shape[0], count_slots
        )
        return jnp.dot(left, kern_y, precision=HIGH).reshape(
            block_depth, kern_x.shape[0], kern_y.shape[1]
        )

    extended = lax.map(block_force, kern_z).reshape(
        levels_dev, rows_dev + 2 * HALO, cols_dev + 2 * HALO
    )
    widened = padded_2(extended, (("gx", 1), ("gy", 2)), HALO)
    force = fold_columns(fold_edges(widened, 1, rows_dev, HALO), cols_dev, HALO)
    columns = rows_dev * cols_dev
    width = 2 * columns
    classes = diff_table.shape[0]
    onehot = (klass.reshape(1, columns) == jnp.arange(classes)[:, None]).astype(jnp.float32)
    table_ext = jnp.concatenate([diff_table, jnp.zeros((classes, 1), jnp.float32)], 1)
    table_window = lax.dynamic_slice_in_dim(table_ext, slab * levels_dev, levels_dev + 1, 1)
    kappa = jnp.dot(table_window.T, onehot, precision=HIGH)
    below = jnp.where(
        global_level[:, None] >= 1, kappa[:levels_dev], jnp.zeros_like(kappa[:levels_dev])
    )
    above = kappa[1:]
    scales = jnp.concatenate(
        [jnp.ones((columns,), jnp.float32), jnp.full((columns,), THETA_SCALE, jnp.float32)]
    )[None, :]
    below_both = jnp.concatenate([below, below], 1)
    above_both = jnp.concatenate([above, above], 1)
    lower = -scales * below_both
    upper = -scales * above_both
    diag = 1.0 + scales * (below_both + above_both)
    rhs = jnp.concatenate(
        [(u_wind + force).reshape(levels_dev, columns), theta.reshape(levels_dev, columns)], 1
    )
    last = levels_dev - 1
    inner_low = lower[1:last].at[0].set(0.0)
    inner_up = upper[1:last].at[-1].set(0.0)
    inner_diag = diag[1:last]
    zeros_inner = jnp.zeros_like(rhs[1:last])
    from_first = zeros_inner.at[0].set(-lower[1])
    from_last = zeros_inner.at[-1].set(-upper[last - 1])
    loads = jnp.concatenate([rhs[1:last], from_first, from_last], 1)
    inner = tridiagonal(
        jnp.concatenate([inner_low] * 3, 1),
        jnp.concatenate([inner_diag] * 3, 1),
        jnp.concatenate([inner_up] * 3, 1),
        loads,
    )
    plain = inner[:, :width]
    resp_first = inner[:, width : 2 * width]
    resp_last = inner[:, 2 * width :]
    first_row = (
        lower[0],
        diag[0] + upper[0] * resp_first[0],
        upper[0] * resp_last[0],
        rhs[0] - upper[0] * plain[0],
    )
    last_row = (
        lower[last] * resp_first[-1],
        diag[last] + lower[last] * resp_last[-1],
        upper[last],
        rhs[last] - lower[last] * plain[-1],
    )
    packed = jnp.stack(first_row + last_row, 0)
    slabs = lax.axis_size("gz")
    every = lax.all_gather(packed[None], "gz", axis=0, tiled=True)
    ordered = every.reshape(2 * slabs, 4, width)
    solved = tridiagonal(ordered[:, 0], ordered[:, 1], ordered[:, 2], ordered[:, 3])
    edge_pair = lax.dynamic_slice_in_dim(solved, 2 * slab, 2, 0)
    first_value = edge_pair[0]
    last_value = edge_pair[1]
    middle = plain + resp_first * first_value[None] + resp_last * last_value[None]
    values = jnp.concatenate([first_value[None], middle, last_value[None]], 0)
    u_next = values[:, :columns].reshape(levels_dev, rows_dev, cols_dev)
    theta_next = values[:, columns:].reshape(levels_dev, rows_dev, cols_dev)
    return (u_next, theta_next)


def solution(mesh):
    return jax.shard_map(
        shards,
        mesh=mesh,
        in_specs=(
            P("gz", "gx", "gy"),
            P("gz", "gx", "gy"),
            P(None, "gx", "gy", None),
            P("gx", "gy"),
            P("gx", "gy"),
            P(),
        ),
        out_specs=(P("gz", "gx", "gy"), P("gz", "gx", "gy")),
        check_vma=False,
    )
```

profile of v0, /device:TPU:4, one launch (start us, length us, event | category | flops | bytes accessed | tf_op | source)
XLA Modules:
  0.0 201.5 jit_solution(2273395250896765318)
XLA Ops:
  2.2 5.4 %while.83 = (s32[]{:T(128)}, f32[4,4,64,128]{3,2,1,0:T(8,128)S(1)}, f32[4,4,1024]{2,1,0:T(4,128)S(1)}, f32[1024]{0:T(1024)S(1)}, f32[64]{0:T(128)S(1)}, /*index=...) while((s32[]{:T(128)}, f32[4,4,64,128]{3,2,1,0:T(8,128)S(1)}, ...), condition=%wide.region_1.2_spmd.clone, body=%wide.region_0.1_spmd.clone.sunk | while | flops 403832832 | bytes 717669 | solution.py:101
  2.4 1.2 fusion.97
  3.7 1.2 fusion.97
  5.1 1.2 fusion.97
  6.5 1.2 fusion.97
  8.4 1.7 collective-permute-start
  10.1 1.3 collective-permute-start.1
  14.5 1.6 pad_maximum_fusion.1
  18.0 3.8 %collective-permute-start.2 = (f32[16,96,16]{1,2,0:T(8,128)S(1)}, f32[16,96,16]{1,2,0:T(8,128)S(1)}, u32[]{:S(2)}, u32[]{:S(2)}) collective-permute-start(f32[16,96,16]{1,2,0:T(8,128)S(1)} %copy.18), channel_id=1, source_target_pairs={{0,4},{4,8},{8,12},{12,16},{16,20},{20,24},{24,28},{28,32},{32,36}... | collective-permute-start | bytes 294920 | tf_op jit(solution)/shard_map/ppermute | solution.py:21
  22.0 1.3 collective-permute-start.3
  24.6 4.4 %collective-permute-done.3 = f32[16,96,16]{1,2,0:T(8,128)} collective-permute-done((f32[16,96,16]{1,2,0:T(8,128)S(1)}, f32[16,96,16]{1,2,0:T(8,128)}, u32[]{:S(2)}, u32[]{:S(2)}) %collective-permute-start.3) | collective-permute-done | bytes 98336 | tf_op jit(solution)/shard_map/ppermute | solution.py:22
  31.1 1.3 convolution_add_fusion
  35.5 89.4 %while.84 = (s32[]{:T(128)}, f32[18432]{0:T(1024)S(1)}, f32[18432]{0:T(1024)S(1)}, f32[14,18432]{1,0:T(8,128)S(1)}, f32[14,18432]{1,0:T(8,128)}, /*index=5*/f32[...) while((s32[]{:T(128)}, f32[18432]{0:T(1024)S(1)}, ...), condition=%wide.region_3.4_spmd.clone, body=%wide.region_2.3_spmd.clone.sunk | while | flops 147459 | bytes 1474695 | solution.py:65
  36.7 1.4 constant_dynamic-slice_fusion.21
  38.1 2.8 %dynamic_update_slice.53 = f32[14,18432]{1,0:T(8,128)} dynamic-update-slice(f32[14,18432]{1,0:T(8,128)} %get-tuple-element.926, f32[1,18432]{1,0:T(1,128)S(1)} %bitcast.95, s32[]{:T(128)} %get-tuple-element.922, s32[]{:T(128)} %constant.249.clone.1..sunk) | dynamic-update-slice | bytes 147460 | tf_op jit(solution)/shard_map/while/body/jit(dynamic_update_index_in_dim)/dynamic_update_slice | solution.py:65
  43.1 1.4 constant_dynamic-slice_fusion.21
  44.5 2.8 %dynamic_update_slice.53 = f32[14,18432]{1,0:T(8,128)} dynamic-update-slice(f32[14,18432]{1,0:T(8,128)} %get-tuple-element.926, f32[1,18432]{1,0:T(1,128)S(1)} %bitcast.95, s32[]{:T(128)} %get-tuple-element.922, s32[]{:T(128)} %constant.249.clone.1..sunk) | dynamic-update-slice | bytes 147460 | tf_op jit(solution)/shard_map/while/body/jit(dynamic_update_index_in_dim)/dynamic_update_slice | solution.py:65
  49.4 1.4 constant_dynamic-slice_fusion.21
  50.9 2.8 %dynamic_update_slice.53 = f32[14,18432]{1,0:T(8,128)} dynamic-update-slice(f32[14,18432]{1,0:T(8,128)} %get-tuple-element.926, f32[1,18432]{1,0:T(1,128)S(1)} %bitcast.95, s32[]{:T(128)} %get-tuple-element.922, s32[]{:T(128)} %constant.249.clone.1..sunk) | dynamic-update-slice | bytes 147460 | tf_op jit(solution)/shard_map/while/body/jit(dynamic_update_index_in_dim)/dynamic_update_slice | solution.py:65
  55.8 1.4 constant_dynamic-slice_fusion.21
  57.3 2.8 %dynamic_update_slice.53 = f32[14,18432]{1,0:T(8,128)} dynamic-update-slice(f32[14,18432]{1,0:T(8,128)} %get-tuple-element.926, f32[1,18432]{1,0:T(1,128)S(1)} %bitcast.95, s32[]{:T(128)} %get-tuple-element.922, s32[]{:T(128)} %constant.249.clone.1..sunk) | dynamic-update-slice | bytes 147460 | tf_op jit(solution)/shard_map/while/body/jit(dynamic_update_index_in_dim)/dynamic_update_slice | solution.py:65
  62.2 1.4 constant_dynamic-slice_fusion.21
  63.6 2.8 %dynamic_update_slice.53 = f32[14,18432]{1,0:T(8,128)} dynamic-update-slice(f32[14,18432]{1,0:T(8,128)} %get-tuple-element.926, f32[1,18432]{1,0:T(1,128)S(1)} %bitcast.95, s32[]{:T(128)} %get-tuple-element.922, s32[]{:T(128)} %constant.249.clone.1..sunk) | dynamic-update-slice | bytes 147460 | tf_op jit(solution)/shard_map/while/body/jit(dynamic_update_index_in_dim)/dynamic_update_slice | solution.py:65
  68.6 1.4 constant_dynamic-slice_fusion.21
  70.0 2.8 %dynamic_update_slice.53 = f32[14,18432]{1,0:T(8,128)} dynamic-update-slice(f32[14,18432]{1,0:T(8,128)} %get-tuple-element.926, f32[1,18432]{1,0:T(1,128)S(1)} %bitcast.95, s32[]{:T(128)} %get-tuple-element.922, s32[]{:T(128)} %constant.249.clone.1..sunk) | dynamic-update-slice | bytes 147460 | tf_op jit(solution)/shard_map/while/body/jit(dynamic_update_index_in_dim)/dynamic_update_slice | solution.py:65
  75.0 1.4 constant_dynamic-slice_fusion.21
  76.4 2.8 %dynamic_update_slice.53 = f32[14,18432]{1,0:T(8,128)} dynamic-update-slice(f32[14,18432]{1,0:T(8,128)} %get-tuple-element.926, f32[1,18432]{1,0:T(1,128)S(1)} %bitcast.95, s32[]{:T(128)} %get-tuple-element.922, s32[]{:T(128)} %constant.249.clone.1..sunk) | dynamic-update-slice | bytes 147460 | tf_op jit(solution)/shard_map/while/body/jit(dynamic_update_index_in_dim)/dynamic_update_slice | solution.py:65
  81.4 1.4 constant_dynamic-slice_fusion.21
  82.8 2.8 %dynamic_update_slice.53 = f32[14,18432]{1,0:T(8,128)} dynamic-update-slice(f32[14,18432]{1,0:T(8,128)} %get-tuple-element.926, f32[1,18432]{1,0:T(1,128)S(1)} %bitcast.95, s32[]{:T(128)} %get-tuple-element.922, s32[]{:T(128)} %constant.249.clone.1..sunk) | dynamic-update-slice | bytes 147460 | tf_op jit(solution)/shard_map/while/body/jit(dynamic_update_index_in_dim)/dynamic_update_slice | solution.py:65
  87.8 1.4 constant_dynamic-slice_fusion.21
  89.2 2.8 %dynamic_update_slice.53 = f32[14,18432]{1,0:T(8,128)} dynamic-update-slice(f32[14,18432]{1,0:T(8,128)} %get-tuple-element.926, f32[1,18432]{1,0:T(1,128)S(1)} %bitcast.95, s32[]{:T(128)} %get-tuple-element.922, s32[]{:T(128)} %constant.249.clone.1..sunk) | dynamic-update-slice | bytes 147460 | tf_op jit(solution)/shard_map/while/body/jit(dynamic_update_index_in_dim)/dynamic_update_slice | solution.py:65
  94.1 1.4 constant_dynamic-slice_fusion.21
  95.6 2.8 %dynamic_update_slice.53 = f32[14,18432]{1,0:T(8,128)} dynamic-update-slice(f32[14,18432]{1,0:T(8,128)} %get-tuple-element.926, f32[1,18432]{1,0:T(1,128)S(1)} %bitcast.95, s32[]{:T(128)} %get-tuple-element.922, s32[]{:T(128)} %constant.249.clone.1..sunk) | dynamic-update-slice | bytes 147460 | tf_op jit(solution)/shard_map/while/body/jit(dynamic_update_index_in_dim)/dynamic_update_slice | solution.py:65
  100.5 1.4 constant_dynamic-slice_fusion.21
  102.0 2.8 %dynamic_update_slice.53 = f32[14,18432]{1,0:T(8,128)} dynamic-update-slice(f32[14,18432]{1,0:T(8,128)} %get-tuple-element.926, f32[1,18432]{1,0:T(1,128)S(1)} %bitcast.95, s32[]{:T(128)} %get-tuple-element.922, s32[]{:T(128)} %constant.249.clone.1..sunk) | dynamic-update-slice | bytes 147460 | tf_op jit(solution)/shard_map/while/body/jit(dynamic_update_index_in_dim)/dynamic_update_slice | solution.py:65
  106.9 1.4 constant_dynamic-slice_fusion.21
  108.3 2.8 %dynamic_update_slice.53 = f32[14,18432]{1,0:T(8,128)} dynamic-update-slice(f32[14,18432]{1,0:T(8,128)} %get-tuple-element.926, f32[1,18432]{1,0:T(1,128)S(1)} %bitcast.95, s32[]{:T(128)} %get-tuple-element.922, s32[]{:T(128)} %constant.249.clone.1..sunk) | dynamic-update-slice | bytes 147460 | tf_op jit(solution)/shard_map/while/body/jit(dynamic_update_index_in_dim)/dynamic_update_slice | solution.py:65
  113.3 1.4 constant_dynamic-slice_fusion.21
  114.7 2.8 %dynamic_update_slice.53 = f32[14,18432]{1,0:T(8,128)} dynamic-update-slice(f32[14,18432]{1,0:T(8,128)} %get-tuple-element.926, f32[1,18432]{1,0:T(1,128)S(1)} %bitcast.95, s32[]{:T(128)} %get-tuple-element.922, s32[]{:T(128)} %constant.249.clone.1..sunk) | dynamic-update-slice | bytes 147460 | tf_op jit(solution)/shard_map/while/body/jit(dynamic_update_index_in_dim)/dynamic_update_slice | solution.py:65
  119.7 1.4 constant_dynamic-slice_fusion.21
  121.1 2.8 %dynamic_update_slice.53 = f32[14,18432]{1,0:T(8,128)} dynamic-update-slice(f32[14,18432]{1,0:T(8,128)} %get-tuple-element.926, f32[1,18432]{1,0:T(1,128)S(1)} %bitcast.95, s32[]{:T(128)} %get-tuple-element.922, s32[]{:T(128)} %constant.249.clone.1..sunk) | dynamic-update-slice | bytes 147460 | tf_op jit(solution)/shard_map/while/body/jit(dynamic_update_index_in_dim)/dynamic_update_slice | solution.py:65
  125.0 31.8 %while.85 = (s32[]{:T(128)}, f32[18432]{0:T(1024)S(1)}, f32[14,18432]{1,0:T(8,128)S(1)}, f32[14,18432]{1,0:T(8,128)}, f32[14,18432]{1,0:T(8,128)S(1)}, /*index=5*/s32[]{:T(128)}, s32[]{:T(128)}, s32[]{:T(128)}) while((s32[]{:T(128)}, f32[18432]{0:T(1024)S(1)}, f32[14,18432]{1,0:T(8,128)S(1)}, f32[14,18432]{1,0:T(8,128)}, ...), condition=%wide.region_5.6_spmd.clone, body=%wide.region_4.5_spmd.clone.sunk | while | flops 55300 | bytes 737395 | solution.py:72
  125.0 1.2 constant_dynamic-slice_fusion.22
  127.3 1.2 constant_dynamic-slice_fusion.22
  156.7 1.6 slice_subtract_fusion
  158.6 23.9 %all-gather = f32[32,6144]{1,0:T(8,128)S(1)} all-gather(f32[8,6144]{1,0:T(8,128)S(1)} %stack.2), channel_id=2, replica_groups=mesh['gx'=8,'gy'=32,'gz'=4] {'gz'}, dimensions={0}, use_global_device_ids=true | all-gather | bytes 983040 | tf_op jit(solution)/shard_map/all_gather | solution.py:159
  183.6 10.5 %while.86 = (s32[]{:T(128)}, f32[6144]{0:T(1024)S(1)}, f32[6144]{0:T(1024)S(1)}, f32[8,6144]{1,0:T(8,128)S(1)}, f32[8,6144]{1,0:T(8,128)S(1)}, /*index=5*/f32[8,...) while((s32[]{:T(128)}, f32[6144]{0:T(1024)S(1)}, ...), condition=%wide.region_7.8_spmd.clone, body=%wide.region_6.7_spmd.clone.sunk | while | flops 49155 | bytes 491655 | solution.py:65
  194.2 5.4 %while.87 = (s32[]{:T(128)}, f32[6144]{0:T(1024)S(1)}, f32[8,6144]{1,0:T(8,128)S(1)}, f32[8,6144]{1,0:T(8,128)S(1)}, f32[8,6144]{1,0:T(8,128)S(1)}, /*index=5*/s32[]{:T(128)}, s32[]{:T(128)}, s32[]{:T(128)}) while((s32[]{:T(128)}, f32[6144]{0:T(1024)S(1)}, f32[8,6144]{1,0:T(8,128)S(1)}, f32[8,6144]{1,0:T(8,128)S(1)}, ...), condition=%wide.region_9.10_spmd.clone, body=%wide.region_8.9_spmd.clone.sunk | while | flops 18436 | bytes 245875 | solution.py:72
  (236 shorter events, 92.0 us)
Async XLA Ops:
  2.2 9.2 %copy-start.5 = (s32[32,96]{1,0:T(8,128)S(1)}, s32[32,96]{1,0:T(8,128)}, u32[]{:S(2)}) copy-start(s32[32,96]{1,0:T(8,128)} %param.28) | copy-start | bytes 36868
  2.2 9.3 %copy-start.6 = (f32[16,64]{1,0:T(8,128)S(1)}, f32[16,64]{1,0:T(8,128)}, u32[]{:S(2)}) copy-start(f32[16,64]{1,0:T(8,128)} %param.29) | copy-start | bytes 12292
  7.7 4.4 %copy-start.3 = (f32[6144]{0:T(1024)S(1)}, f32[6144]{0:T(1024)}, u32[]{:S(2)}) copy-start(f32[6144]{0:T(1024)} %constant.251.clone.1) | copy-start | bytes 73732
  7.7 4.4 %copy-start.4 = (f32[6144]{0:T(1024)S(1)}, f32[6144]{0:T(1024)}, u32[]{:S(2)}) copy-start(f32[6144]{0:T(1024)} %constant.256.clone.1) | copy-start | bytes 73732
  8.4 9.0 %collective-permute-start = (f32[16,16,128]{2,1,0:T(8,128)}, f32[16,16,128]{2,1,0:T(8,128)S(1)}, u32[]{:S(2)}, u32[]{:S(2)}) collective-permute-start(f32[16,16,128]{2,1,0:T(8,128)} %get-tuple-element.606), channel_id=1, source_target_pairs={{0,128},{128,256},{256,384},{384,512},{512,640},{640,768},{768,896... | collective-permute-start | bytes 393224 | tf_op jit(solution)/shard_map/ppermute | solution.py:21
  10.1 7.2 %collective-permute-start.1 = (f32[16,16,128]{2,1,0:T(8,128)}, f32[16,16,128]{2,1,0:T(8,128)S(1)}, u32[]{:S(2)}, u32[]{:S(2)}) collective-permute-start(f32[16,16,128]{2,1,0:T(8,128)} %get-tuple-element.607), channel_id=1, source_target_pairs={{128,0},{256,128},{384,256},{512,384},{640,512},{768,640},{896,768... | collective-permute-start | bytes 393224 | tf_op jit(solution)/shard_map/ppermute | solution.py:22
  12.1 4.0 %copy-start = (f32[16,6144]{1,0:T(8,128)}, f32[16,6144]{1,0:T(8,128)S(1)}, u32[]{:S(2)}) copy-start(f32[16,6144]{1,0:T(8,128)S(1)} %get-tuple-element.618) | copy-start | bytes 1179652
  12.2 4.0 %copy-start.1 = (f32[16,6144]{1,0:T(8,128)}, f32[16,6144]{1,0:T(8,128)S(1)}, u32[]{:S(2)}) copy-start(f32[16,6144]{1,0:T(8,128)S(1)} %get-tuple-element.617) | copy-start | bytes 1179652
  18.0 6.3 %collective-permute-start.2 = (f32[16,96,16]{1,2,0:T(8,128)S(1)}, f32[16,96,16]{1,2,0:T(8,128)S(1)}, u32[]{:S(2)}, u32[]{:S(2)}) collective-permute-start(f32[16,96,16]{1,2,0:T(8,128)S(1)} %copy.18), channel_id=1, source_target_pairs={{0,4},{4,8},{8,12},{12,16},{16,20},{20,24},{24,28},{28,32},{32,36}... | collective-permute-start | bytes 294920 | tf_op jit(solution)/shard_map/ppermute | solution.py:21
  22.0 7.0 %collective-permute-start.3 = (f32[16,96,16]{1,2,0:T(8,128)S(1)}, f32[16,96,16]{1,2,0:T(8,128)}, u32[]{:S(2)}, u32[]{:S(2)}) collective-permute-start(f32[16,96,16]{1,2,0:T(8,128)S(1)} %copy.19), channel_id=1, source_target_pairs={{4,0},{8,4},{12,8},{16,12},{20,16},{24,20},{28,24},{32,28},{36,32}... | collective-permute-start | bytes 294920 | tf_op jit(solution)/shard_map/ppermute | solution.py:22
  30.2 1.0 copy-start.7
  30.2 0.9 copy-start.8
  33.6 0.8 copy-start.2
where the time goes:
time: 205 us; the launch traced here: 202 us
  local copies, waits for them, and re-layouts  146 us (71%)
  blocking collectives  23.9 us (12%)
  starting transfers between devices  8.15 us (4%)
  other arithmetic  7.73 us (4%)
  matrix products  6.4 us (3%)
  waiting for transfers between devices  5.39 us (3%)
    dynamic_update_slice x66, local copies, waits for them, and re-layouts, tridiagonal(): _, (mods, rights) = lax.scan(forward, start, (lower, diag, upper, rhs))  80.9 us
    dynamic_slice x66, local copies, waits for them, and re-layouts, tridiagonal(): _, (mods, rights) = lax.scan(forward, start, (lower, diag, upper, rhs))  52.7 us
    all_gather x1, blocking collectives, shards(): every = lax.all_gather(packed[None], 'gz', axis=0, tiled=True)  23.9 us
    ppermute x2, starting transfers between devices, padded_2(): before = lax.ppermute(last, axis, up)  5.56 us
    dot_general x4, matrix products, block_force(): jnp.dot(left, kern_y, precision=HIGH)  4.74 us
    ppermute x2, waiting for transfers between devices, padded_2(): after = lax.ppermute(first, axis, down)  4.44 us
  transfers between devices with their start and end apart: 4, of which 2 were waited for; matrix products, arithmetic and copies ran while one was open for 3% of the time, Pallas kernels for 0%

commit v1 on v0

v1 whole, which is shorter than its diff:
```python
import functools
import math

import jax
import jax.numpy as jnp
from jax import lax
from jax.experimental import pallas as pl
from jax.experimental.pallas import tpu as pltpu
from jax.sharding import PartitionSpec as P

HALO = 16
THETA_SCALE = 1.25
CLASSES = 16
LANES = 128
STRAIGHT = ((-1, 0), (1, 0), (0, -1), (0, 1))
DIAGONAL = ((-1, -1), (1, 1), (1, -1), (-1, 1))
TILES = STRAIGHT + DIAGONAL
SPARE = len(TILES)
ACROSS = (2, 3, 4, 5, 6, 7)
NT = (((1,), (1,)), ((), ()))
VMEM_LIMIT = 48 * 1024 * 1024


def lane_iota(shape):
    return lax.broadcasted_iota(jnp.int32, shape, len(shape) - 1)


def gauss(coords, centres):
    offset = (coords - centres) * (2.0 / HALO * math.sqrt(math.log2(math.e)))
    return jnp.exp2(-(offset * offset))


def halves(value):
    high = value.astype(jnp.bfloat16)
    return high, (value - high.astype(jnp.float32)).astype(jnp.bfloat16)


def whole_blocks(live, size):
    return lax.div(live + (size - 1), size)


def pick(table_row, index):
    return jnp.take_along_axis(jnp.broadcast_to(table_row, index.shape), index, axis=1, mode="promise_in_bounds")


def pack_columns(full):
    tail = full[24:32]
    lane = lane_iota((8, LANES))
    parts = []
    for part in range(3):
        moved = pltpu.roll(tail, 96 - 32 * part, 1)
        parts.append(jnp.where(lane < 96, full[8 * part : 8 * part + 8], moved))
    return jnp.concatenate(parts, 0)


def unpack_columns(dense):
    lane = lane_iota((8, LANES))
    first = pltpu.roll(dense[0:8], 32, 1)
    second = pltpu.roll(dense[8:16], 64, 1)
    third = pltpu.roll(dense[16:24], 96, 1)
    tail = jnp.where(lane < 32, first, jnp.where(lane < 64, second, third))
    return jnp.concatenate([dense, tail], 0)


def widen(ref_value):
    rows, cols = ref_value.shape
    return jnp.concatenate([ref_value, jnp.zeros((rows, LANES - cols), ref_value.dtype)], 1)


def column_tables(depth, levels, slabs, table_ref, up_ref, down_ref, mix_ref, inv_ref, square_ref):
    slab = lax.axis_index("gz")
    inv_ref[...] = 1.0 / table_ref[...]
    value = jnp.ones((1, LANES), jnp.float32)
    flux = value
    high = value
    back = value
    up_ref[0:1, :] = value
    down_ref[depth - 1 : depth, :] = high
    for step in range(1, depth):
        value = value + flux * inv_ref[step : step + 1, :]
        flux = flux + value
        up_ref[step : step + 1, :] = value
        other = depth - 1 - step
        high = high + back * inv_ref[other + 1 : other + 2, :]
        back = back + high
        down_ref[other : other + 1, :] = high
    down_ref[...] = down_ref[...] * (1.0 / flux)
    level = lax.broadcasted_iota(jnp.int32, (depth, LANES), 0)
    lane = lane_iota((depth, LANES))
    below = jnp.where(level < slab * levels, up_ref[...], 0.0)
    above = jnp.where(level >= (slab + 1) * levels, down_ref[...], 0.0)
    mixed = jnp.where(lane < CLASSES, below, pltpu.roll(above, CLASSES, 1))
    square_ref[0:depth, :] = mixed
    square_ref[depth:LANES, :] = jnp.zeros((LANES - depth, LANES), jnp.float32)
    mix_ref[...] = jnp.transpose(square_ref[...])[0 : 2 * CLASSES, :]


def send_kernel(points_hbm, count_ref, out_ref, sem):
    points = pltpu.make_async_copy(points_hbm, out_ref.at[0:32], sem)
    points.start()
    out_ref[32:40, :] = count_ref[...].astype(jnp.float32)
    points.wait()


def own_kernel(slabs, u_hbm, theta_hbm, klass_hbm, table_ref, sent_ref,
               sums_ref, up_ref, down_ref, mix_ref, index_ref, acc_ref,
               inv_ref, square_ref, u_ref, theta_ref, klass_ref, sems):
    levels, rows, cols = u_ref.shape
    depth = levels * slabs
    slab = lax.axis_index("gz")
    copies = [
        pltpu.make_async_copy(source, target, sems.at[number])
        for number, (source, target) in enumerate(
            ((klass_hbm, klass_ref), (u_hbm, u_ref), (theta_hbm, theta_ref))
        )
    ]
    for copy in copies:
        copy.start()
    live = jnp.max(sent_ref[32:40, :]).astype(jnp.int32)
    column_tables(depth, levels, slabs, table_ref, up_ref, down_ref, mix_ref, inv_ref, square_ref)
    acc_ref[...] = jnp.zeros_like(acc_ref)
    mix = mix_ref[:, 0:depth]

    def chunk(c, carry):
        entries = [(0, 4 * c + k, live, 0, 0) for k in range(4)]
        add_points(sent_ref, entries, mix, acc_ref, 0, rows, False, cols)
        return carry

    lax.fori_loop(0, whole_blocks(live, 4 * LANES), chunk, 0)
    for copy in copies:
        copy.wait()
    index = widen(klass_ref[...])
    index_ref[...] = index
    zero = jnp.zeros(index.shape, jnp.float32)
    sums = [zero, zero, zero, zero]
    start = pl.multiple_of(slab * levels, levels)
    ups = up_ref[pl.ds(start, levels), :]
    downs = down_ref[pl.ds(start, levels), :]
    for z in range(levels):
        u_rows = widen(u_ref[z])
        t_rows = widen(theta_ref[z])
        sums[0] = sums[0] + pick(ups[z : z + 1], index) * u_rows
        sums[1] = sums[1] + pick(ups[z : z + 1], index + CLASSES) * t_rows
        sums[2] = sums[2] + pick(downs[z : z + 1], index) * u_rows
        sums[3] = sums[3] + pick(downs[z : z + 1], index + CLASSES) * t_rows
    for number, part in enumerate(sums):
        sums_ref[24 * number : 24 * number + 24, :] = pack_columns(part)


def pack_kernel(slabs, sums_ref, straight_ref, diagonal_ref, out_ref):
    slab = lax.axis_index("gz")
    counts = jnp.where(lane_iota((8, LANES)) < LANES // 2, straight_ref[32:40, :], diagonal_ref[32:40, :])
    for target in range(slabs):
        out_ref[target, 0:48, :] = jnp.where(target > slab, sums_ref[0:48, :], sums_ref[48:96, :])
        out_ref[target, 48:80, :] = straight_ref[0:32, :]
        out_ref[target, 80:112, :] = diagonal_ref[0:32, :]
        out_ref[target, 112:120, :] = counts


def heights(points_ref, entries, mix, levels):
    slab = lax.axis_index("gz")
    depth = mix.shape[1]
    places = []
    parts = []
    for base, which, live, _, _ in entries:
        px, py, pz, weight = (points_ref[pl.ds(base + 8 * a + which, 1), :] for a in range(4))
        weight = jnp.where(which * LANES + lane_iota((1, LANES)) < live, weight, 0.0)
        places.append((px, py, weight))
        z = lax.broadcasted_iota(jnp.int32, (depth, LANES), 0)
        own = slab * levels + lax.broadcasted_iota(jnp.int32, (levels, LANES), 0)
        parts.append((gauss(z.astype(jnp.float32), pz), gauss(own.astype(jnp.float32), pz)))
    gz, own = (jnp.concatenate(both, 1) for both in zip(*parts))
    other = jnp.dot(mix, gz, precision=lax.Precision.HIGHEST, preferred_element_type=jnp.float32)
    return places, jnp.concatenate([own, other], 0)


def add_points(points_ref, entries, mix, acc_ref, first_row, n_rows, masked, cols):
    deep, rows, _ = acc_ref.shape
    tile_x, tile_y = (lax.axis_index(name) for name in ("gx", "gy"))
    places, high = heights(points_ref, entries, mix, deep - 2 * CLASSES)
    i = tile_x * rows + first_row + lax.broadcasted_iota(jnp.int32, (n_rows, LANES), 0)
    j = tile_y * cols + lax.broadcasted_iota(jnp.int32, (cols, LANES), 0)
    parts = []
    for (px, py, weight), (_, _, _, at_x, _) in zip(places, entries):
        gi = gauss(i.astype(jnp.float32), px)
        if masked:
            inner = i - (at_x * rows - HALO)
            gi = jnp.where((inner >= 0) & (inner < rows + 2 * HALO), gi, 0.0)
        parts.append((gi, gauss(j.astype(jnp.float32), py) * weight))
    gi, gj = (jnp.concatenate(both, 1) for both in zip(*parts))
    width = gi.shape[1]
    right_high, right_low = halves(gj)
    gap = jnp.zeros((LANES - cols, width), jnp.bfloat16)
    right_high = jnp.concatenate([right_high, gap], 0)
    right = jnp.concatenate([right_high, right_low, gap], 0)
    block = 2 * LANES // n_rows
    for first in range(0, deep, block):
        left = (high[first : first + block, None, :] * gi[None]).reshape(block * n_rows, width)
        left_high, left_low = halves(left)
        wide = lax.dot_general(left_high, right, NT, preferred_element_type=jnp.float32)
        narrow = lax.dot_general(left_low, right_high, NT, preferred_element_type=jnp.float32)
        total = wide[:, :LANES] + wide[:, LANES:] + narrow
        acc_ref[first : first + block, first_row : first_row + n_rows, :] += total.reshape(block, n_rows, LANES)


def add_across(points_ref, entries, mix, side_ref, rows, cols):
    deep = side_ref.shape[0]
    tile_x, tile_y = (lax.axis_index(name) for name in ("gx", "gy"))
    places, high = heights(points_ref, entries, mix, deep - 2 * CLASSES)
    i = tile_x * rows + lax.broadcasted_iota(jnp.int32, (rows, LANES), 0)
    column = lax.broadcasted_iota(jnp.int32, (HALO, LANES), 0)
    parts = []
    for (px, py, weight), (_, _, _, at_x, at_y) in zip(places, entries):
        before = at_y < tile_y
        j = tile_y * cols + jnp.where(before, 0, cols - HALO) + column
        inner = i - (at_x * rows - HALO)
        gi = gauss(i.astype(jnp.float32), px)
        gi = jnp.where((inner >= 0) & (inner < rows + 2 * HALO), gi, 0.0)
        gi = jnp.concatenate([jnp.where(before, gi, 0.0), jnp.where(before, 0.0, gi)], 0)
        parts.append((gauss(j.astype(jnp.float32), py) * weight, gi))
    gj, gi = (jnp.concatenate(both, 1) for both in zip(*parts))
    width = gi.shape[1]
    right_high, right_low = halves(gi)
    right = jnp.concatenate([right_high, right_low], 0)
    right_high = jnp.concatenate([right_high, jnp.zeros_like(right_high)], 0)
    block = 2 * LANES // HALO
    for first in range(0, deep, block):
        left = (high[first : first + block, None, :] * gj[None]).reshape(block * HALO, width)
        left_high, left_low = halves(left)
        total = lax.dot_general(left_high, right, NT, preferred_element_type=jnp.float32)
        total = total + lax.dot_general(left_low, right_high, NT, preferred_element_type=jnp.float32)
        side_ref[first : first + block] += total.reshape(block, HALO, LANES)


def by_class(value_of, index):
    low = jnp.zeros(index.shape, jnp.float32)
    high = low
    for c in range(CLASSES):
        here = index == c
        low = jnp.where(here, value_of(c), low)
        high = jnp.where(here, value_of(CLASSES + c), high)
    return low, high


def side_fields(side_ref, index_ref, stack_ref, rows, cols):
    levels = side_ref.shape[0] - 2 * CLASSES
    square = jnp.concatenate([index_ref[...], jnp.zeros((LANES - rows, LANES), jnp.int32)], 0)
    square = jnp.transpose(square.astype(jnp.float32))
    first = square[0:HALO]
    last = pltpu.roll(square[cols - HALO : cols], rows, 1)
    index = jnp.where(lane_iota(first.shape) < rows, first, last).astype(jnp.int32)

    def folded(z):
        return side_ref[z] + pltpu.roll(side_ref[z], 2 * rows, 1)

    for z in range(levels):
        stack_ref[z * HALO : (z + 1) * HALO, :] = folded(z)
    low, high = by_class(lambda c: folded(levels + c), index)
    stack_ref[levels * HALO : (levels + 1) * HALO, :] = low
    stack_ref[(levels + 1) * HALO : (levels + 2) * HALO, :] = high
    lane = lane_iota((rows, LANES))
    fields = []
    per = LANES // HALO
    for group in range(stack_ref.shape[0] // LANES):
        turned = jnp.transpose(stack_ref[group * LANES : (group + 1) * LANES, :])
        for k in range(per):
            if group * per + k < levels + 2:
                before = pltpu.roll(turned[0:rows], (LANES - k * HALO) % LANES, 1)
                after = pltpu.roll(turned[rows : 2 * rows], (LANES + cols - HALO - k * HALO) % LANES, 1)
                fields.append(jnp.where(lane < HALO, before, jnp.where((lane >= cols - HALO) & (lane < cols), after, 0.0)))
    return fields


def solve_field(in_ref, index, ups, downs, low, high, force_of, out_ref, gather_ref, copy_of):
    levels, _, cols = in_ref.shape
    for z in range(levels):
        right = force_of(z, widen(in_ref[z]))
        up = pick(ups[z : z + 1], index)
        down = pick(downs[z : z + 1], index)
        low = low + up * right
        gather_ref[0, z] = down * low
        gather_ref[1, z] = up
        gather_ref[2, z] = down * right
    for z in range(levels - 1, -1, -1):
        out_ref[z] = (gather_ref[0, z] + gather_ref[1, z] * high)[:, :cols]
        high = high + gather_ref[2, z]
        if z == levels // 2:
            copy_of(1).start()
    copy_of(0).start()


def last_kernel(slabs, got_ref, own_ref, u_hbm, theta_hbm, index_ref, up_ref, down_ref, mix_ref, u_out, theta_out,
                acc_ref, points_ref, side_ref, stack_ref, gather_ref, u_ref, theta_ref, u_new, theta_new,
                live_ref, at_ref, list_ref, sems, out_sems):
    levels, rows, cols = u_ref.shape
    copies = [
        pltpu.make_async_copy(theta_hbm, theta_ref, sems.at[0]),
        pltpu.make_async_copy(u_hbm, u_ref, sems.at[1]),
    ]
    for copy in copies:
        copy.start()

    def out_copy(field, half):
        source, target = ((u_new, u_out), (theta_new, theta_out))[field]
        part = pl.ds(half * (levels // 2), levels // 2)
        return pltpu.make_async_copy(source.at[part], target.at[part], out_sems.at[field, half])

    tile_x, tile_y, slab = (lax.axis_index(name) for name in ("gx", "gy", "gz"))
    depth = levels * slabs
    mix = mix_ref[:, 0:depth]
    lane8 = lane_iota((8, LANES))
    low_sum = jnp.zeros((48, LANES), jnp.float32)
    high_sum = low_sum
    for source in range(slabs):
        points_ref[source * 32 : source * 32 + 32, :] = got_ref[source, 48:80, :]
        points_ref[(source + slabs) * 32 : (source + slabs) * 32 + 32, :] = got_ref[source, 80:112, :]
        counts = got_ref[source, 112:120, :]
        live_ref[source] = jnp.max(jnp.where(lane8 < LANES // 2, counts, 0.0)).astype(jnp.int32)
        live_ref[source + slabs] = jnp.max(jnp.where(lane8 < LANES // 2, 0.0, counts)).astype(jnp.int32)
        edge = got_ref[source, 0:48, :]
        low_sum = low_sum + jnp.where(source < slab, edge, 0.0)
        high_sum = high_sum + jnp.where(source > slab, edge, 0.0)
    points_ref[SPARE * 32 : SPARE * 32 + 32, :] = jnp.zeros((32, LANES), jnp.float32)
    live_ref[SPARE] = 0
    for number, (dx, dy) in enumerate(TILES + ((0, 1),)):
        at_ref[2 * number] = tile_x + dx
        at_ref[2 * number + 1] = tile_y + dy

    index = index_ref[...]
    start = pl.multiple_of(slab * levels, levels)
    ups = up_ref[pl.ds(start, levels), :]
    downs = down_ref[pl.ds(start, levels), :]
    copies[0].wait()
    solve_field(theta_ref, index + CLASSES, ups, downs, unpack_columns(low_sum[24:48]), unpack_columns(high_sum[24:48]),
                lambda z, right: right, theta_new, gather_ref, functools.partial(out_copy, 1))

    acc_ref[...] = own_ref[...]
    for number, first_row in ((0, 0), (1, rows - HALO)):
        live = live_ref[number]

        def chunk(c, carry):
            entries = [(number * 32, 2 * c + k, live, at_ref[2 * number], at_ref[2 * number + 1]) for k in range(2)]
            add_points(points_ref, entries, mix, acc_ref, first_row, HALO, True, cols)
            return carry

        lax.fori_loop(0, whole_blocks(live, 2 * LANES), chunk, 0)

    filled = jnp.int32(0)
    for number in ACROSS:
        def note(k, carry):
            list_ref[filled + k] = number * 8 + k
            return carry

        blocks = whole_blocks(live_ref[number], LANES)
        lax.fori_loop(0, blocks, note, 0)
        filled = filled + blocks
    list_ref[filled] = SPARE * 8
    side_ref[...] = jnp.zeros_like(side_ref)
    stack_ref[...] = jnp.zeros_like(stack_ref)

    def pair(c, carry):
        entries = []
        for k in range(2):
            entry = list_ref[2 * c + k]
            number = lax.shift_right_logical(entry, 3)
            entries.append((number * 32, lax.bitwise_and(entry, 7), live_ref[number], at_ref[2 * number],
                            at_ref[2 * number + 1]))
        add_across(points_ref, entries, mix, side_ref, rows, cols)
        return carry

    lax.fori_loop(0, whole_blocks(filled, 2), pair, 0)
    fields = side_fields(side_ref, index_ref, stack_ref, rows, cols)
    low_force, high_force = by_class(lambda c: acc_ref[levels + c], index)
    copies[1].wait()
    solve_field(u_ref, index, ups, downs,
                unpack_columns(low_sum[0:24]) + low_force + fields[levels],
                unpack_columns(high_sum[0:24]) + high_force + fields[levels + 1],
                lambda z, right: right + acc_ref[z] + fields[z], u_new, gather_ref, functools.partial(out_copy, 0))
    for field in range(2):
        for half in range(2):
            out_copy(field, half).wait()


def lateral(offsets, tiles_x, tiles_y, slabs):
    pairs = []
    for x in range(tiles_x):
        for y in range(tiles_y):
            for t in range(slabs):
                sx, sy = x + offsets[t][0], y + offsets[t][1]
                if 0 <= sx < tiles_x and 0 <= sy < tiles_y:
                    pairs.append(((sx * tiles_y + sy) * slabs + t, (x * tiles_y + y) * slabs + t))
    return pairs


def shards(u_wind, theta, act_points, point_count, klass, diff_table):
    levels, rows, cols = u_wind.shape
    tiles_x, tiles_y, slabs = (lax.axis_size(name) for name in ("gx", "gy", "gz"))
    depth = levels * slabs
    f32 = jnp.float32
    stay = lambda x: pltpu.with_memory_space_constraint(x, pltpu.HBM)
    u_wind, theta, klass = stay(u_wind), stay(theta), stay(klass)
    vmem = pl.BlockSpec(memory_space=pltpu.VMEM)
    hbm = pl.BlockSpec(memory_space=pltpu.HBM)
    params = pltpu.CompilerParams(vmem_limit_bytes=VMEM_LIMIT)
    sent = pl.pallas_call(
        send_kernel,
        out_shape=jax.ShapeDtypeStruct((40, LANES), f32),
        in_specs=[hbm, vmem],
        out_specs=vmem,
        scratch_shapes=[pltpu.SemaphoreType.DMA],
        compiler_params=params,
        name="send",
    )(stay(act_points.reshape(32, LANES)), jnp.broadcast_to(point_count, (8, LANES)))
    axes = ("gx", "gy", "gz")
    straight = lax.ppermute(sent, axes, lateral(STRAIGHT, tiles_x, tiles_y, slabs))
    diagonal = lax.ppermute(sent, axes, lateral(DIAGONAL, tiles_x, tiles_y, slabs))
    table = diff_table.T
    table = jnp.concatenate([table, THETA_SCALE * table, jnp.ones((depth, LANES - 2 * CLASSES), f32)], 1)
    acc_shape = (levels + 2 * CLASSES, rows, LANES)
    field = pltpu.VMEM(u_wind.shape, f32)
    sums, ups, downs, mix, index, own = pl.pallas_call(
        functools.partial(own_kernel, slabs),
        out_shape=[
            jax.ShapeDtypeStruct((96, LANES), f32),
            jax.ShapeDtypeStruct((depth, LANES), f32),
            jax.ShapeDtypeStruct((depth, LANES), f32),
            jax.ShapeDtypeStruct((2 * CLASSES, LANES), f32),
            jax.ShapeDtypeStruct((rows, LANES), jnp.int32),
            jax.ShapeDtypeStruct(acc_shape, f32),
        ],
        in_specs=[hbm, hbm, hbm, vmem, vmem],
        out_specs=[vmem] * 6,
        scratch_shapes=[
            pltpu.VMEM((depth, LANES), f32),
            pltpu.VMEM((LANES, LANES), f32),
            field,
            field,
            pltpu.VMEM((rows, cols), jnp.int32),
            pltpu.SemaphoreType.DMA((3,)),
        ],
        compiler_params=params,
        cost_estimate=pl.CostEstimate(flops=2 * 10**9, bytes_accessed=10**6, transcendentals=10**5),
        name="own_tile",
    )(u_wind, theta, klass, table, sent)
    packed = pl.pallas_call(
        functools.partial(pack_kernel, slabs),
        out_shape=jax.ShapeDtypeStruct((slabs, 120, LANES), f32),
        compiler_params=params,
        name="pack",
    )(sums, straight, diagonal)
    got = lax.all_to_all(packed, "gz", 0, 0)
    return pl.pallas_call(
        functools.partial(last_kernel, slabs),
        out_shape=[jax.ShapeDtypeStruct(u_wind.shape, f32)] * 2,
        in_specs=[vmem, vmem, hbm, hbm, vmem, vmem, vmem, vmem],
        out_specs=[hbm] * 2,
        scratch_shapes=[
            pltpu.VMEM(acc_shape, f32),
            pltpu.VMEM(((SPARE + 1) * 32, LANES), f32),
            pltpu.VMEM((levels + 2 * CLASSES, HALO, LANES), f32),
            pltpu.VMEM((3 * LANES, LANES), f32),
            pltpu.VMEM((3, levels, rows, LANES), f32),
            field,
            field,
            field,
            field,
            pltpu.SMEM((SPARE + 1,), jnp.int32),
            pltpu.SMEM((2 * SPARE + 2,), jnp.int32),
            pltpu.SMEM((8 * SPARE,), jnp.int32),
            pltpu.SemaphoreType.DMA((2,)),
            pltpu.SemaphoreType.DMA((2, 2)),
        ],
        compiler_params=params,
        name="solve",
    )(got, own, u_wind, theta, index, ups, downs, mix)


def solution(mesh):
    return jax.shard_map(
        shards,
        mesh=mesh,
        in_specs=(
            P("gz", "gx", "gy"),
            P("gz", "gx", "gy"),
            P(None, "gx", "gy", None),
            P("gx", "gy"),
            P("gx", "gy"),
            P(),
        ),
        out_specs=(P("gz", "gx", "gy"), P("gz", "gx", "gy")),
        check_vma=False,
    )
```

time: 205 us -> 36.5 us (0.18)
  the two profiles are of different devices: /device:TPU:4 before, /device:TPU:225 now
where the time goes in v1:
time: 36.5 us; the launch traced here: 36.2 us
  Pallas kernels  14.9 us (41%)
  blocking collectives  11.5 us (32%)
  starting transfers between devices  8.25 us (23%)
  between operations  1.36 us (4%)
    pallas_call x1, Pallas kernels, shards(): pl.pallas_call(functools.partial(last_kernel, slabs), out_shape=[jax.Shap...  11.8 us
    all_to_all x1, blocking collectives, shards(): got = lax.all_to_all(packed, 'gz', 0, 0)  11.5 us
    ppermute x1, starting transfers between devices, shards(): lax.ppermute(sent, axes, lateral(DIAGONAL, tiles_x, tiles_y, slabs))  6.33 us
    pallas_call x1, Pallas kernels, shards(): pl.pallas_call(functools.partial(own_kernel, slabs), out_shape=[jax.Shape...  2.33 us
    ppermute x1, starting transfers between devices, shards(): lax.ppermute(sent, axes, lateral(STRAIGHT, tiles_x, tiles_y, slabs))  1.92 us
    pallas_call x1, Pallas kernels, shards(): pl.pallas_call(send_kernel, out_shape=jax.ShapeDtypeStruct((40, LANES), f...  0.73 us
  transfers between devices with their start and end apart: 2, of which 0 were waited for; matrix products, arithmetic and copies ran while one was open for 1% of the time, Pallas kernels for 6%

profile of v1, /device:TPU:225, one launch (start us, length us, event | category | flops | bytes accessed | tf_op | source)
XLA Modules:
  0.0 36.2 jit_solution(484351896303192963)
XLA Ops:
  1.3 0.0 copy-start
  1.3 0.7 %send.1.sent_ref = f32[40,128]{1,0:T(8,128)S(1)} custom-call(f32[32,128]{1,0:T(8,128)} %bitcast.6, s32[8,128]{1,0:T(8,128)S(1)} %broadcast_in_dim.12.count_ref), custom_call_target="tpu_custom_call" | custom-call | tf_op jit(solution)/shard_map/send/pallas_call | solution.py:405
  2.0 6.3 %collective-permute-start.1 = (f32[40,128]{1,0:T(8,128)S(1)}, f32[40,128]{1,0:T(8,128)S(1)}, u32[]{:S(2)}, u32[]{:S(2)}) collective-permute-start(f32[40,128]{1,0:T(8,128)S(1)} %send.1.sent_ref), channel_id=1, source_target_pairs={{133,1},{137,5},{130,6},{141,9},{134,10},{145,13},{138,14},{149,17... | collective-permute-start | bytes 61448 | tf_op jit(solution)/shard_map/ppermute | solution.py:416
  8.4 1.9 %collective-permute-start = (f32[40,128]{1,0:T(8,128)S(1)}, f32[40,128]{1,0:T(8,128)S(1)}, u32[]{:S(2)}, u32[]{:S(2)}) collective-permute-start(f32[40,128]{1,0:T(8,128)S(1)} %send.1.sent_ref), channel_id=1, source_target_pairs={{129,1},{7,3},{133,5},{2,6},{11,7},{137,9},{6,10},{15,11},{141,13}... | collective-permute-start | bytes 61448 | tf_op jit(solution)/shard_map/ppermute | solution.py:415
  10.3 0.0 copy-done
  10.3 0.1 copy.8
  10.4 0.1 pad.2.clone
  10.5 0.1 maximum_maximum_fusion.table_ref
  10.6 2.3 %own_tile.1 = (f32[96,128]{1,0:T(8,128)S(1)}, f32[64,128]{1,0:T(8,128)S(1)}, f32[64,128]{1,0:T(8,128)S(1)}, f32[32,128]{1,0:T(8,128)S(1)}, s32[32,128]{1,0:T(8,128)S(1)}, /*index=5*/f32[48,32,128]{2,1,0:T(8,128)S(1)}) custom-call(f32[16,32,96]{2,1,0:T(8,128)} %u_hbm.3, f32[16,32,96]{2,1,0:T(8,128)} %theta_hbm.3, s32[32,96]{1,0:T(8,128)} %klass_hbm.1, ...), custom_call_target="tpu_custom_call" | custom-call | flops 2000000000 | bytes 1000000 | tf_op jit(solution)/shard_map/own_tile/pallas_call | solution.py:421
  12.9 0.0 collective-permute-done.1.diagonal_ref
  12.9 0.0 collective-permute-done.straight_ref
  13.0 11.5 %all_to_all.5.got_ref = f32[4,120,128]{2,1,0:T(8,128)S(1)} all-to-all(f32[4,120,128]{2,1,0:T(8,128)S(1)} %pack.1), channel_id=1, replica_groups=mesh['gx'=8,'gy'=32,'gz'=4] {'gz'}, dimensions={0} | all-to-all | bytes 491520 | tf_op jit(solution)/shard_map/all_to_all | solution.py:451
  24.4 11.8 %solve.1 = (f32[16,32,96]{2,1,0:T(8,128)}, f32[16,32,96]{2,1,0:T(8,128)}) custom-call(f32[4,120,128]{2,1,0:T(8,128)S(1)} %all_to_all.5.got_ref, f32[48,32,128]{2,1,0:T(8,128)S(1)} %get-tuple-element.9.own_ref, f32[16,32,96]{2,1,0:T(8,128)} %u_hbm.3, f32[16,32,96]{2,1,0:T(8,128)} %theta_hbm.3, s32[32,128]{1,0:T(8,128)S(1)} %get-tuple-element.10.index_ref, ...), custom_call_target="tpu_custom_call" | custom-call | tf_op jit(solution)/shard_map/solve/pallas_call | solution.py:452
  (4 shorter events, 0.0 us)
Async XLA Ops:
  1.3 9.0 %copy-start = (f32[16,64]{1,0:T(8,128)S(1)}, f32[16,64]{1,0:T(8,128)}, u32[]{:S(2)}) copy-start(f32[16,64]{1,0:T(8,128)} %param.11) | copy-start | bytes 12292
  2.0 10.9 %collective-permute-start.1 = (f32[40,128]{1,0:T(8,128)S(1)}, f32[40,128]{1,0:T(8,128)S(1)}, u32[]{:S(2)}, u32[]{:S(2)}) collective-permute-start(f32[40,128]{1,0:T(8,128)S(1)} %send.1.sent_ref), channel_id=1, source_target_pairs={{133,1},{137,5},{130,6},{141,9},{134,10},{145,13},{138,14},{149,17... | collective-permute-start | bytes 61448 | tf_op jit(solution)/shard_map/ppermute | solution.py:416
  8.4 4.5 %collective-permute-start = (f32[40,128]{1,0:T(8,128)S(1)}, f32[40,128]{1,0:T(8,128)S(1)}, u32[]{:S(2)}, u32[]{:S(2)}) collective-permute-start(f32[40,128]{1,0:T(8,128)S(1)} %send.1.sent_ref), channel_id=1, source_target_pairs={{129,1},{7,3},{133,5},{2,6},{11,7},{137,9},{6,10},{15,11},{141,13}... | collective-permute-start | bytes 61448 | tf_op jit(solution)/shard_map/ppermute | solution.py:415

commit v2 on v1

v2 whole, which is shorter than its diff:
```python
import functools
import math

import jax
import jax.numpy as jnp
from jax import lax
from jax.experimental import pallas as pl
from jax.experimental.pallas import tpu as pltpu
from jax.sharding import PartitionSpec as P

HALO = 16
THETA_SCALE = 1.25
CLASSES = 16
LANES = 128
STRAIGHT = ((-1, 0), (1, 0), (0, -1), (0, 1))
DIAGONAL = ((-1, -1), (1, 1), (1, -1), (-1, 1))
TILES = STRAIGHT + DIAGONAL
SPARE = len(TILES)
PIECES = 4
FINE = HALO // 2
LOG2E = math.log2(math.e)
MANY = 8
ACROSS = (2, 3, 4, 5, 6, 7)
NT = (((1,), (1,)), ((), ()))
VMEM_LIMIT = 48 * 1024 * 1024


def lane_iota(shape):
    return lax.broadcasted_iota(jnp.int32, shape, len(shape) - 1)


def gauss(coords, centres):
    offset = (coords - centres) * (2.0 / HALO * math.sqrt(LOG2E))
    return jnp.exp2(-(offset * offset))


def halves(value):
    high = value.astype(jnp.bfloat16)
    return high, (value - high.astype(jnp.float32)).astype(jnp.bfloat16)


def mix_halves(mix_ref, depth):
    high, low = halves(mix_ref[...])
    low = pltpu.roll(low.astype(jnp.float32), depth, 1)
    both = jnp.where(lane_iota(low.shape) < depth, high.astype(jnp.float32), low).astype(jnp.bfloat16)
    return jnp.concatenate([both, high[:, :depth]], 1)


def whole_blocks(live, size):
    return lax.div(live + (size - 1), size)


def in_batches(blocks, add):
    done = jnp.int32(0)
    for size in (MANY, MANY // 2, MANY // 4):
        spare = size // 2 - 1 if size > MANY // 4 else size - 1
        steps = lax.div(blocks - done + spare, size)

        def batch(c, carry, done=done, size=size):
            add(done + size * c, size)
            return carry

        lax.fori_loop(0, steps, batch, 0)
        done = jnp.minimum(done + size * steps, blocks)


def pick(table_row, index):
    return jnp.take_along_axis(jnp.broadcast_to(table_row, index.shape), index, axis=1, mode="promise_in_bounds")


def pack_columns(full):
    tail = full[24:32]
    lane = lane_iota((8, LANES))
    parts = []
    for part in range(3):
        moved = pltpu.roll(tail, 96 - 32 * part, 1)
        parts.append(jnp.where(lane < 96, full[8 * part : 8 * part + 8], moved))
    return jnp.concatenate(parts, 0)


def unpack_columns(dense):
    lane = lane_iota((8, LANES))
    first = pltpu.roll(dense[0:8], 32, 1)
    second = pltpu.roll(dense[8:16], 64, 1)
    third = pltpu.roll(dense[16:24], 96, 1)
    tail = jnp.where(lane < 32, first, jnp.where(lane < 64, second, third))
    return jnp.concatenate([dense, tail], 0)


def widen(ref_value):
    rows, cols = ref_value.shape
    return jnp.concatenate([ref_value, jnp.zeros((rows, LANES - cols), ref_value.dtype)], 1)


def column_tables(depth, levels, slabs, table_ref, up_ref, down_ref, mix_ref, inv_ref, square_ref):
    slab = lax.axis_index("gz")
    square_ref[...] = jnp.ones((LANES, LANES), jnp.float32)
    square_ref[0:CLASSES, 0:depth] = table_ref[...]
    square_ref[CLASSES : 2 * CLASSES, 0:depth] = THETA_SCALE * table_ref[...]
    inv_ref[...] = 1.0 / jnp.transpose(square_ref[...])[0:depth]
    value = jnp.ones((1, LANES), jnp.float32)
    flux = value
    high = value
    back = value
    up_ref[0:1, :] = value
    down_ref[depth - 1 : depth, :] = high
    for step in range(1, depth):
        value = value + flux * inv_ref[step : step + 1, :]
        flux = flux + value
        up_ref[step : step + 1, :] = value
        other = depth - 1 - step
        high = high + back * inv_ref[other + 1 : other + 2, :]
        back = back + high
        down_ref[other : other + 1, :] = high
    down_ref[...] = down_ref[...] * (1.0 / flux)
    level = lax.broadcasted_iota(jnp.int32, (depth, LANES), 0)
    lane = lane_iota((depth, LANES))
    below = jnp.where(level < slab * levels, up_ref[...], 0.0)
    above = jnp.where(level >= (slab + 1) * levels, down_ref[...], 0.0)
    mixed = jnp.where(lane < CLASSES, below, pltpu.roll(above, CLASSES, 1))
    square_ref[0:depth, :] = mixed
    square_ref[depth:LANES, :] = jnp.zeros((LANES - depth, LANES), jnp.float32)
    mix_ref[...] = jnp.transpose(square_ref[...])[0 : 2 * CLASSES, :]


def own_kernel(slabs, u_hbm, theta_hbm, klass_hbm, table_ref, sent_ref,
               sums_ref, mix_ref, index_ref, acc_ref, u_ref, theta_ref, picks_ref,
               up_ref, down_ref, inv_ref, square_ref, klass_ref, sems):
    levels, rows, cols = u_ref.shape
    depth = levels * slabs
    slab = lax.axis_index("gz")
    part = levels // PIECES
    copies = [pltpu.make_async_copy(klass_hbm, klass_ref, sems.at[0])]
    for piece in range(PIECES):
        at = pl.ds(piece * part, part)
        copies.append(pltpu.make_async_copy(u_hbm.at[at], u_ref.at[at], sems.at[1 + 2 * piece]))
        copies.append(pltpu.make_async_copy(theta_hbm.at[at], theta_ref.at[at], sems.at[2 + 2 * piece]))
    for copy in copies:
        copy.start()
    live = jnp.max(sent_ref[32:40, :]).astype(jnp.int32)
    column_tables(depth, levels, slabs, table_ref, up_ref, down_ref, mix_ref, inv_ref, square_ref)
    acc_ref[...] = jnp.zeros_like(acc_ref)
    mix = mix_halves(mix_ref, depth)

    def add(first, n):
        entries = [(0, first + k, live, 0, 0) for k in range(n)]
        add_points(sent_ref, entries, mix, acc_ref, tuple(range(rows // FINE)), cols)

    in_batches(whole_blocks(live, LANES), add)
    copies[0].wait()
    index = widen(klass_ref[...])
    index_ref[...] = index
    zero = jnp.zeros(index.shape, jnp.float32)
    start = pl.multiple_of(slab * levels, levels)
    ups = up_ref[pl.ds(start, levels), :]
    downs = down_ref[pl.ds(start, levels), :]
    for z in range(levels):
        picks_ref[0, z] = pick(ups[z : z + 1], index)
        picks_ref[1, z] = pick(ups[z : z + 1], index + CLASSES)
        picks_ref[2, z] = pick(downs[z : z + 1], index)
        picks_ref[3, z] = pick(downs[z : z + 1], index + CLASSES)
    sums = [zero, zero, zero, zero]
    for copy in copies[1:]:
        copy.wait()
    for z in range(levels):
        u_rows = widen(u_ref[z])
        t_rows = widen(theta_ref[z])
        sums[0] = sums[0] + picks_ref[0, z] * u_rows
        sums[1] = sums[1] + picks_ref[1, z] * t_rows
        sums[2] = sums[2] + picks_ref[2, z] * u_rows
        sums[3] = sums[3] + picks_ref[3, z] * t_rows
    for number, part in enumerate(sums):
        sums_ref[24 * number : 24 * number + 24, :] = pack_columns(part)


def pack_kernel(slabs, sums_ref, straight_ref, diagonal_ref, out_ref):
    slab = lax.axis_index("gz")
    counts = straight_ref[32:40, :] + pltpu.roll(diagonal_ref[32:40, :], LANES // 2, 1)
    for target in range(slabs):
        out_ref[target, 0:48, :] = jnp.where(target > slab, sums_ref[0:48, :], sums_ref[48:96, :])
        out_ref[target, 48:80, :] = straight_ref[0:32, :]
        out_ref[target, 80:112, :] = diagonal_ref[0:32, :]
        out_ref[target, 112:120, :] = counts


def heights(points_ref, entries, mix, levels):
    slab = lax.axis_index("gz")
    depth = mix.shape[1] // 3
    places = []
    parts = []
    for base, which, live, _, _ in entries:
        px, py, pz, weight = (points_ref[pl.ds(base + 8 * a + which, 1), :] for a in range(4))
        alive = which * LANES + lane_iota((1, LANES)) < live
        places.append((px, py, jnp.where(alive, weight, 0.0), alive))
        z = lax.broadcasted_iota(jnp.int32, (depth, LANES), 0)
        own = slab * levels + lax.broadcasted_iota(jnp.int32, (levels, LANES), 0)
        parts.append((gauss(z.astype(jnp.float32), pz), gauss(own.astype(jnp.float32), pz)))
    gz, own = (jnp.concatenate(both, 1) for both in zip(*parts))
    gz_high, gz_low = halves(gz)
    other = jnp.dot(mix, jnp.concatenate([gz_high, gz_high, gz_low], 0), preferred_element_type=jnp.float32)
    return places, jnp.concatenate([own, other], 0)


def left_halves(high, fine):
    deep, width = high.shape
    return halves((high[:, None, :] * fine[None]).reshape(deep * FINE, width))


def fine_and_coarse(place, steps):
    cell = lax.broadcasted_iota(jnp.int32, (FINE,) + place.shape[1:], 0).astype(jnp.float32)
    fine = gauss(cell, place)
    coarse = [jnp.exp2(LOG2E * (2.0 * step / FINE * place - float(step * step))) for step in steps]
    return fine, coarse


def add_points(points_ref, entries, mix, acc_ref, steps, cols):
    deep, rows, _ = acc_ref.shape
    tile_x, tile_y = (lax.axis_index(name) for name in ("gx", "gy"))
    places, high = heights(points_ref, entries, mix, deep - 2 * CLASSES)
    j = lax.broadcasted_iota(jnp.int32, (cols, LANES), 0).astype(jnp.float32)
    parts = []
    for px, py, weight, alive in places:
        x = jnp.where(alive, px - (tile_x * rows).astype(jnp.float32), 0.0)
        fine, coarse = fine_and_coarse(x, steps)
        gj = gauss(j, py - (tile_y * cols).astype(jnp.float32))
        parts.append([fine, gj] + [factor * weight for factor in coarse])
    fine, gj, *coarse = (jnp.concatenate(both, 1) for both in zip(*parts))
    gap = jnp.zeros((LANES - cols, gj.shape[1]), jnp.bfloat16)
    pairs = [halves(gj * factor) for factor in coarse]
    right_high = jnp.concatenate([x for pair in pairs for x in (pair[0], gap)], 0)
    right_low = jnp.concatenate([x for pair in pairs for x in (pair[1], gap)], 0)
    left_high, left_low = left_halves(high, fine)
    left = jnp.concatenate([left_high, left_low, left_high], 1)
    right = jnp.concatenate([right_high, right_high, right_low], 1)
    total = lax.dot_general(left, right, NT, preferred_element_type=jnp.float32)
    for number, step in enumerate(steps):
        part = total[:, number * LANES : (number + 1) * LANES].reshape(deep, FINE, LANES)
        acc_ref[:, step * FINE : (step + 1) * FINE, :] += part


def add_sides(points_ref, entries, mix, side_ref, rows, cols):
    deep = side_ref.shape[0]
    tile_x, tile_y = (lax.axis_index(name) for name in ("gx", "gy"))
    places, high = heights(points_ref, entries, mix, deep - 2 * CLASSES)
    i = lax.broadcasted_iota(jnp.int32, (rows, LANES), 0)
    parts = []
    for (px, py, weight, alive), (_, _, _, at_x, at_y) in zip(places, entries):
        before = at_y < tile_y
        y = py - (tile_y * cols).astype(jnp.float32)
        y = jnp.where(alive, jnp.where(before, y, float(cols - 1) - y), 0.0)
        fine, coarse = fine_and_coarse(y, (0, 1))
        backward = gauss(float(FINE - 1) - lax.broadcasted_iota(jnp.int32, fine.shape, 0).astype(jnp.float32), y)
        inner = i - ((at_x - tile_x) * rows - HALO)
        gi = gauss(i.astype(jnp.float32), px - (tile_x * rows).astype(jnp.float32)) * weight
        gi = jnp.where((inner >= 0) & (inner < rows + 2 * HALO), gi, 0.0)
        gi = jnp.concatenate([jnp.where(before, gi, 0.0), jnp.where(before, 0.0, gi)], 0)
        parts.append((jnp.where(before, fine, backward), gi, coarse[0], coarse[1]))
    fine, gi, *coarse = (jnp.concatenate(both, 1) for both in zip(*parts))
    right_high, right_low = halves(jnp.concatenate([gi * factor for factor in coarse], 0))
    right = jnp.concatenate(
        [jnp.concatenate([right_high, right_low], 0), jnp.concatenate([right_high, jnp.zeros_like(right_low)], 0)], 1
    )
    left = jnp.concatenate(left_halves(high, fine), 1)
    total = lax.dot_general(left, right, NT, preferred_element_type=jnp.float32)
    side_ref[...] += (total[:, :LANES] + total[:, LANES:]).reshape(side_ref.shape)


def cross_factor(step, cell):
    return jnp.exp2((-2.0 * LOG2E / FINE) * (step * cell).astype(jnp.float32))


def by_class(value_of, index):
    low = jnp.zeros(index.shape, jnp.float32)
    high = low
    for c in range(CLASSES):
        here = index == c
        low = jnp.where(here, value_of(c), low)
        high = jnp.where(here, value_of(CLASSES + c), high)
    return low, high


def side_fields(side_ref, index_ref, stack_ref, rows, cols):
    levels = side_ref.shape[0] - 2 * CLASSES
    square = jnp.concatenate([index_ref[...], jnp.zeros((LANES - rows, LANES), jnp.int32)], 0)
    square = jnp.transpose(square.astype(jnp.float32))
    first = square[0:HALO]
    last = pltpu.roll(square[cols - HALO : cols], rows, 1)
    index = jnp.where(lane_iota(first.shape) < rows, first, last).astype(jnp.int32)

    lane = lane_iota((FINE, LANES))
    line = lax.broadcasted_iota(jnp.int32, (FINE, LANES), 0)
    on_first = lane % (2 * rows) < rows
    cross = cross_factor(lane // (2 * rows), jnp.where(on_first, line, FINE - 1 - line))

    def folded(z):
        near = side_ref[z] * cross
        far = pltpu.roll(near, 2 * rows, 1)
        return jnp.concatenate([jnp.where(lane < rows, near, far), jnp.where(lane < rows, far, near)], 0)

    for z in range(levels):
        stack_ref[z * HALO : (z + 1) * HALO, :] = folded(z)
    low, high = by_class(lambda c: folded(levels + c), index)
    stack_ref[levels * HALO : (levels + 1) * HALO, :] = low
    stack_ref[(levels + 1) * HALO : (levels + 2) * HALO, :] = high
    wide = lane_iota((rows, LANES))
    fields = []
    per = LANES // HALO
    for group in range(stack_ref.shape[0] // LANES):
        turned = jnp.transpose(stack_ref[group * LANES : (group + 1) * LANES, :])
        for k in range(per):
            if group * per + k < levels + 2:
                before = pltpu.roll(turned[0:rows], (LANES - k * HALO) % LANES, 1)
                after = pltpu.roll(turned[rows : 2 * rows], (LANES + cols - HALO - k * HALO) % LANES, 1)
                fields.append(jnp.where(wide < HALO, before, jnp.where((wide >= cols - HALO) & (wide < cols), after, 0.0)))
    return fields


def solve_field(in_ref, picks_ref, field, low, high, force_of, out_ref, gather_ref, copy_of):
    levels, _, cols = in_ref.shape
    for z in range(levels):
        right = force_of(z, widen(in_ref[z]))
        down = picks_ref[2 + field, z]
        low = low + picks_ref[field, z] * right
        gather_ref[0, z] = down * low
        gather_ref[1, z] = down * right
    for z in range(levels - 1, -1, -1):
        out_ref[z] = (gather_ref[0, z] + picks_ref[field, z] * high)[:, :cols]
        high = high + gather_ref[1, z]
        if z % (levels // PIECES) == 0:
            copy_of(z // (levels // PIECES)).start()


def last_kernel(slabs, got_ref, own_ref, u_ref, theta_ref, index_ref, picks_ref, mix_ref, u_out, theta_out,
                acc_ref, points_ref, side_ref, stack_ref, gather_ref, u_new, theta_new,
                live_ref, at_ref, list_ref, out_sems):
    levels, rows, cols = u_ref.shape

    def out_copy(field, piece):
        source, target = ((u_new, u_out), (theta_new, theta_out))[field]
        part = pl.ds(piece * (levels // PIECES), levels // PIECES)
        return pltpu.make_async_copy(source.at[part], target.at[part], out_sems.at[field, piece])

    tile_x, tile_y, slab = (lax.axis_index(name) for name in ("gx", "gy", "gz"))
    depth = levels * slabs
    mix = mix_halves(mix_ref, depth)
    lane8 = lane_iota((8, LANES))
    low_sum = jnp.zeros((48, LANES), jnp.float32)
    high_sum = low_sum
    for source in range(slabs):
        points_ref[source * 32 : source * 32 + 32, :] = got_ref[source, 48:80, :]
        points_ref[(source + slabs) * 32 : (source + slabs) * 32 + 32, :] = got_ref[source, 80:112, :]
        counts = got_ref[source, 112:120, :]
        live_ref[source] = jnp.max(jnp.where(lane8 < LANES // 2, counts, 0.0)).astype(jnp.int32)
        live_ref[source + slabs] = jnp.max(jnp.where(lane8 < LANES // 2, 0.0, counts)).astype(jnp.int32)
        edge = got_ref[source, 0:48, :]
        low_sum = low_sum + jnp.where(source < slab, edge, 0.0)
        high_sum = high_sum + jnp.where(source > slab, edge, 0.0)
    points_ref[SPARE * 32 : SPARE * 32 + 32, :] = jnp.zeros((32, LANES), jnp.float32)
    live_ref[SPARE] = 0
    for number, (dx, dy) in enumerate(TILES + ((0, 1),)):
        at_ref[2 * number] = tile_x + dx
        at_ref[2 * number + 1] = tile_y + dy

    index = index_ref[...]
    solve_field(theta_ref, picks_ref, 1, unpack_columns(low_sum[24:48]), unpack_columns(high_sum[24:48]),
                lambda z, right: right, theta_new, gather_ref, functools.partial(out_copy, 1))

    acc_ref[...] = own_ref[...]
    for number, steps in ((0, (0, 1)), (1, (rows // FINE - 2, rows // FINE - 1))):
        live = live_ref[number]

        def add(first, n):
            entries = [(number * 32, first + k, live, 0, 0) for k in range(n)]
            add_points(points_ref, entries, mix, acc_ref, steps, cols)

        in_batches(whole_blocks(live, LANES), add)

    filled = jnp.int32(0)
    for number in ACROSS:
        for k in range(8):
            list_ref[filled + k] = number * 8 + k
        filled = filled + whole_blocks(live_ref[number], LANES)
    for k in range(MANY):
        list_ref[filled + k] = SPARE * 8
    side_ref[...] = jnp.zeros_like(side_ref)
    stack_ref[...] = jnp.zeros_like(stack_ref)

    def add_side(first, n):
        entries = []
        for k in range(n):
            entry = list_ref[first + k]
            number = lax.shift_right_logical(entry, 3)
            entries.append((number * 32, lax.bitwise_and(entry, 7), live_ref[number], at_ref[2 * number],
                            at_ref[2 * number + 1]))
        add_sides(points_ref, entries, mix, side_ref, rows, cols)

    in_batches(filled, add_side)
    fields = side_fields(side_ref, index_ref, stack_ref, rows, cols)
    row = lax.broadcasted_iota(jnp.int32, (rows, LANES), 0)
    cross = cross_factor(row // FINE, row % FINE)
    low_force, high_force = by_class(lambda c: acc_ref[levels + c], index)
    solve_field(u_ref, picks_ref, 0,
                unpack_columns(low_sum[0:24]) + low_force * cross + fields[levels],
                unpack_columns(high_sum[0:24]) + high_force * cross + fields[levels + 1],
                lambda z, right: right + acc_ref[z] * cross + fields[z], u_new, gather_ref, functools.partial(out_copy, 0))
    for field in range(2):
        for piece in range(PIECES):
            out_copy(field, piece).wait()


def lateral(offsets, tiles_x, tiles_y, slabs):
    pairs = []
    for x in range(tiles_x):
        for y in range(tiles_y):
            for t in range(slabs):
                sx, sy = x + offsets[t][0], y + offsets[t][1]
                if 0 <= sx < tiles_x and 0 <= sy < tiles_y:
                    pairs.append(((sx * tiles_y + sy) * slabs + t, (x * tiles_y + y) * slabs + t))
    return pairs


def shards(u_wind, theta, act_points, point_count, klass, diff_table):
    levels, rows, cols = u_wind.shape
    tiles_x, tiles_y, slabs = (lax.axis_size(name) for name in ("gx", "gy", "gz"))
    depth = levels * slabs
    f32 = jnp.float32
    stay = lambda x: pltpu.with_memory_space_constraint(x, pltpu.HBM)
    u_wind, theta, klass = stay(u_wind), stay(theta), stay(klass)
    vmem = pl.BlockSpec(memory_space=pltpu.VMEM)
    hbm = pl.BlockSpec(memory_space=pltpu.HBM)
    params = pltpu.CompilerParams(vmem_limit_bytes=VMEM_LIMIT)
    count = jnp.pad(point_count.astype(f32), ((0, 7), (0, LANES - 1)))
    sent = jnp.concatenate([act_points.reshape(32, LANES), count], 0)
    axes = ("gx", "gy", "gz")
    straight = lax.ppermute(sent, axes, lateral(STRAIGHT, tiles_x, tiles_y, slabs))
    diagonal = lax.ppermute(sent, axes, lateral(DIAGONAL, tiles_x, tiles_y, slabs))
    acc_shape = (levels + 2 * CLASSES, rows, LANES)
    field = pltpu.VMEM(u_wind.shape, f32)
    sums, mix, index, own, u_here, theta_here, picks = pl.pallas_call(
        functools.partial(own_kernel, slabs),
        out_shape=[
            jax.ShapeDtypeStruct((96, LANES), f32),
            jax.ShapeDtypeStruct((2 * CLASSES, LANES), f32),
            jax.ShapeDtypeStruct((rows, LANES), jnp.int32),
            jax.ShapeDtypeStruct(acc_shape, f32),
            jax.ShapeDtypeStruct(u_wind.shape, f32),
            jax.ShapeDtypeStruct(u_wind.shape, f32),
            jax.ShapeDtypeStruct((4, levels, rows, LANES), f32),
        ],
        in_specs=[hbm, hbm, hbm, vmem, vmem],
        out_specs=[vmem] * 7,
        scratch_shapes=[
            pltpu.VMEM((depth, LANES), f32),
            pltpu.VMEM((depth, LANES), f32),
            pltpu.VMEM((depth, LANES), f32),
            pltpu.VMEM((LANES, LANES), f32),
            pltpu.VMEM((rows, cols), jnp.int32),
            pltpu.SemaphoreType.DMA((1 + 2 * PIECES,)),
        ],
        compiler_params=params,
        cost_estimate=pl.CostEstimate(flops=2 * 10**9, bytes_accessed=10**6, transcendentals=10**5),
        name="own_tile",
    )(u_wind, theta, klass, diff_table, sent)
    packed = pl.pallas_call(
        functools.partial(pack_kernel, slabs),
        out_shape=jax.ShapeDtypeStruct((slabs, 120, LANES), f32),
        compiler_params=params,
        name="pack",
    )(sums, straight, diagonal)
    got = lax.all_to_all(packed, "gz", 0, 0)
    return pl.pallas_call(
        functools.partial(last_kernel, slabs),
        out_shape=[jax.ShapeDtypeStruct(u_wind.shape, f32)] * 2,
        in_specs=[vmem] * 7,
        out_specs=[hbm] * 2,
        scratch_shapes=[
            pltpu.VMEM(acc_shape, f32),
            pltpu.VMEM(((SPARE + 1) * 32, LANES), f32),
            pltpu.VMEM((levels + 2 * CLASSES, FINE, LANES), f32),
            pltpu.VMEM((3 * LANES, LANES), f32),
            pltpu.VMEM((2, levels, rows, LANES), f32),
            field,
            field,
            pltpu.SMEM((SPARE + 1,), jnp.int32),
            pltpu.SMEM((2 * SPARE + 2,), jnp.int32),
            pltpu.SMEM((8 * SPARE,), jnp.int32),
            pltpu.SemaphoreType.DMA((2, PIECES)),
        ],
        compiler_params=params,
        name="solve",
    )(got, own, u_here, theta_here, index, picks, mix)


def solution(mesh):
    return jax.shard_map(
        shards,
        mesh=mesh,
        in_specs=(
            P("gz", "gx", "gy"),
            P("gz", "gx", "gy"),
            P(None, "gx", "gy", None),
            P("gx", "gy"),
            P("gx", "gy"),
            P(),
        ),
        out_specs=(P("gz", "gx", "gy"), P("gz", "gx", "gy")),
        check_vma=False,
    )
```

time: 36.5 us -> 31.7 us (0.87)
  the two profiles are of different devices: /device:TPU:225 before, /device:TPU:2 now
where the time goes in v2:
time: 31.7 us; the launch traced here: 31.4 us
  blocking collectives  20.7 us (65%)
  Pallas kernels  6.06 us (19%)
  starting transfers between devices  2.57 us (8%)
  between operations  1.33 us (4%)
  other arithmetic  0.73 us (2%)
    all_to_all x1, blocking collectives, shards(): got = lax.all_to_all(packed, 'gz', 0, 0)  20.7 us
    pallas_call x1, Pallas kernels, shards(): pl.pallas_call(functools.partial(own_kernel, slabs), out_shape=[jax.Shape...  3.22 us
    pallas_call x1, Pallas kernels, shards(): pl.pallas_call(functools.partial(last_kernel, slabs), out_shape=[jax.Shap...  2.77 us
    ppermute x1, starting transfers between devices, shards(): lax.ppermute(sent, axes, lateral(STRAIGHT, tiles_x, tiles_y, slabs))  1.29 us
    ppermute x1, starting transfers between devices, shards(): lax.ppermute(sent, axes, lateral(DIAGONAL, tiles_x, tiles_y, slabs))  1.28 us
    concatenate x1, other arithmetic, shards(): sent = jnp.concatenate([act_points.reshape(32, LANES), count], 0)  0.73 us
  transfers between devices with their start and end apart: 2, of which 0 were waited for; matrix products, arithmetic and copies ran while one was open for 0% of the time, Pallas kernels for 10%

profile of v2, /device:TPU:2, one launch (start us, length us, event | category | flops | bytes accessed | tf_op | source)
XLA Modules:
  0.0 31.4 jit_solution(12963802199487088840)
XLA Ops:
  1.3 0.0 copy-start
  1.3 0.7 %select_maximum_fusion.sent_ref = f32[40,128]{1,0:T(8,128)S(1)} fusion(f32[1,1]{1,0:T(1,128)S(6)} %convert_element_type.5, f32[32,128]{1,0:T(8,128)} %bitcast.1), kind=kLoop, calls=%fused_computation | loop fusion | flops 15360 | bytes 36868 | tf_op jit(solution)/shard_map/concatenate | solution.py:433
  2.0 1.3 %collective-permute-start.1 = (f32[40,128]{1,0:T(8,128)S(1)}, f32[40,128]{1,0:T(8,128)S(1)}, u32[]{:S(2)}, u32[]{:S(2)}) collective-permute-start(f32[40,128]{1,0:T(8,128)S(1)} %select_maximum_fusion.sent_ref), channel_id=1, source_target_pairs={{133,1},{137,5},{130,6},{141,9},{134,10},{145,13},{138,14},{149,17... | collective-permute-start | bytes 61448 | tf_op jit(solution)/shard_map/ppermute | solution.py:436
  3.3 1.3 %collective-permute-start = (f32[40,128]{1,0:T(8,128)S(1)}, f32[40,128]{1,0:T(8,128)S(1)}, u32[]{:S(2)}, u32[]{:S(2)}) collective-permute-start(f32[40,128]{1,0:T(8,128)S(1)} %select_maximum_fusion.sent_ref), channel_id=1, source_target_pairs={{129,1},{7,3},{133,5},{2,6},{11,7},{137,9},{6,10},{15,11},{141,13}... | collective-permute-start | bytes 61448 | tf_op jit(solution)/shard_map/ppermute | solution.py:435
  4.6 0.0 copy-done
  4.6 3.2 %own_tile.1 = (f32[96,128]{1,0:T(8,128)S(1)}, f32[32,128]{1,0:T(8,128)S(1)}, s32[32,128]{1,0:T(8,128)S(1)}, f32[48,32,128]{2,1,0:T(8,128)S(1)}, f32[16,32,96]{2,...) custom-call(f32[16,32,96]{2,1,0:T(8,128)} %u_hbm.1, f32[16,32,96]{2,1,0:T(8,128)} %theta_hbm.1, ...), custom_call_target="tpu_custom_call" | custom-call | flops 2000000000 | bytes 1000000 | tf_op jit(solution)/shard_map/own_tile/pallas_call | solution.py:439
  7.8 0.0 collective-permute-done.1.diagonal_ref
  7.8 0.0 collective-permute-done.straight_ref
  7.9 0.1 pack.1
  7.9 20.7 %all_to_all.5.got_ref = f32[4,120,128]{2,1,0:T(8,128)S(1)} all-to-all(f32[4,120,128]{2,1,0:T(8,128)S(1)} %pack.1), channel_id=1, replica_groups=mesh['gx'=8,'gy'=32,'gz'=4] {'gz'}, dimensions={0} | all-to-all | bytes 491520 | tf_op jit(solution)/shard_map/all_to_all | solution.py:470
  28.6 2.8 %solve.1 = (f32[16,32,96]{2,1,0:T(8,128)}, f32[16,32,96]{2,1,0:T(8,128)}) custom-call(f32[4,120,128]{2,1,0:T(8,128)S(1)} %all_to_all.5.got_ref, f32[48,32,128]{2,1,0:T(8,128)S(1)} %get-tuple-element.10.own_ref, f32[16,32,96]{2,1,0:T(8,128)S(1)} %get-tuple-element.11.u_ref, f32[16,32,96]{2,1,0:T(8,128)S(1)} %get-tuple-element.12.theta_ref, ...), custom_call_target="tpu_custom_call" | custom-call | tf_op jit(solution)/shard_map/solve/pallas_call | solution.py:471
Async XLA Ops:
  1.3 3.3 %copy-start = (f32[16,64]{1,0:T(8,128)S(1)}, f32[16,64]{1,0:T(8,128)}, u32[]{:S(2)}) copy-start(f32[16,64]{1,0:T(8,128)} %table_ref.1) | copy-start | bytes 12292
  2.0 5.8 %collective-permute-start.1 = (f32[40,128]{1,0:T(8,128)S(1)}, f32[40,128]{1,0:T(8,128)S(1)}, u32[]{:S(2)}, u32[]{:S(2)}) collective-permute-start(f32[40,128]{1,0:T(8,128)S(1)} %select_maximum_fusion.sent_ref), channel_id=1, source_target_pairs={{133,1},{137,5},{130,6},{141,9},{134,10},{145,13},{138,14},{149,17... | collective-permute-start | bytes 61448 | tf_op jit(solution)/shard_map/ppermute | solution.py:436
  3.3 4.5 %collective-permute-start = (f32[40,128]{1,0:T(8,128)S(1)}, f32[40,128]{1,0:T(8,128)S(1)}, u32[]{:S(2)}, u32[]{:S(2)}) collective-permute-start(f32[40,128]{1,0:T(8,128)S(1)} %select_maximum_fusion.sent_ref), channel_id=1, source_target_pairs={{129,1},{7,3},{133,5},{2,6},{11,7},{137,9},{6,10},{15,11},{141,13}... | collective-permute-start | bytes 61448 | tf_op jit(solution)/shard_map/ppermute | solution.py:435

commit v3 on v2

--- a/solution.py
+++ b/solution.py
@@ -123,9 +123,24 @@
     mix_ref[...] = jnp.transpose(square_ref[...])[0 : 2 * CLASSES, :]
 
 
+def solve_field(in_ref, picks_ref, field, low, high, force_of, out_ref, gather_ref, copy_of):
+    levels, _, cols = in_ref.shape
+    for z in range(levels):
+        right = force_of(z, widen(in_ref[z]))
+        down = picks_ref[2 + field, z]
+        low = low + picks_ref[field, z] * right
+        gather_ref[0, z] = down * low
+        gather_ref[1, z] = down * right
+    for z in range(levels - 1, -1, -1):
+        out_ref[z] = (gather_ref[0, z] + picks_ref[field, z] * high)[:, :cols]
+        high = high + gather_ref[1, z]
+        if copy_of is not None and z % (levels // PIECES) == 0:
+            copy_of(z // (levels // PIECES)).start()
+
+
 def own_kernel(slabs, u_hbm, theta_hbm, klass_hbm, table_ref, sent_ref,
                sums_ref, mix_ref, index_ref, acc_ref, u_ref, theta_ref, picks_ref,
-               up_ref, down_ref, inv_ref, square_ref, klass_ref, sems):
+               up_ref, down_ref, inv_ref, square_ref, klass_ref, gather_ref, sems):
     levels, rows, cols = u_ref.shape
     depth = levels * slabs
     slab = lax.axis_index("gz")
@@ -171,6 +186,7 @@
         sums[3] = sums[3] + picks_ref[3, z] * t_rows
     for number, part in enumerate(sums):
         sums_ref[24 * number : 24 * number + 24, :] = pack_columns(part)
+    solve_field(theta_ref, picks_ref, 1, zero, zero, lambda z, right: right, theta_ref, gather_ref, None)
 
 
 def pack_kernel(slabs, sums_ref, straight_ref, diagonal_ref, out_ref):
@@ -315,21 +331,6 @@
     return fields
 
 
-def solve_field(in_ref, picks_ref, field, low, high, force_of, out_ref, gather_ref, copy_of):
-    levels, _, cols = in_ref.shape
-    for z in range(levels):
-        right = force_of(z, widen(in_ref[z]))
-        down = picks_ref[2 + field, z]
-        low = low + picks_ref[field, z] * right
-        gather_ref[0, z] = down * low
-        gather_ref[1, z] = down * right
-    for z in range(levels - 1, -1, -1):
-        out_ref[z] = (gather_ref[0, z] + picks_ref[field, z] * high)[:, :cols]
-        high = high + gather_ref[1, z]
-        if z % (levels // PIECES) == 0:
-            copy_of(z // (levels // PIECES)).start()
-
-
 def last_kernel(slabs, got_ref, own_ref, u_ref, theta_ref, index_ref, picks_ref, mix_ref, u_out, theta_out,
                 acc_ref, points_ref, side_ref, stack_ref, gather_ref, u_new, theta_new,
                 live_ref, at_ref, list_ref, out_sems):
@@ -362,8 +363,13 @@
         at_ref[2 * number + 1] = tile_y + dy
 
     index = index_ref[...]
-    solve_field(theta_ref, picks_ref, 1, unpack_columns(low_sum[24:48]), unpack_columns(high_sum[24:48]),
-                lambda z, right: right, theta_new, gather_ref, functools.partial(out_copy, 1))
+    low = unpack_columns(low_sum[24:48])[:, :cols]
+    high = unpack_columns(high_sum[24:48])[:, :cols]
+    for z in range(levels):
+        other = picks_ref[3, z][:, :cols] * low + picks_ref[1, z][:, :cols] * high
+        theta_new[z] = theta_ref[z] + other
+        if (z + 1) % (levels // PIECES) == 0:
+            out_copy(1, z // (levels // PIECES)).start()
 
     acc_ref[...] = own_ref[...]
     for number, steps in ((0, (0, 1)), (1, (rows // FINE - 2, rows // FINE - 1))):
@@ -429,8 +435,8 @@
     vmem = pl.BlockSpec(memory_space=pltpu.VMEM)
     hbm = pl.BlockSpec(memory_space=pltpu.HBM)
     params = pltpu.CompilerParams(vmem_limit_bytes=VMEM_LIMIT)
-    count = jnp.pad(point_count.astype(f32), ((0, 7), (0, LANES - 1)))
-    sent = jnp.concatenate([act_points.reshape(32, LANES), count], 0)
+    sent = jnp.pad(act_points.reshape(32, LANES), ((0, 8), (0, 0)))
+    sent = lax.dynamic_update_slice(sent, point_count.astype(f32), (32 + lax.axis_index("gz"), 0))
     axes = ("gx", "gy", "gz")
     straight = lax.ppermute(sent, axes, lateral(STRAIGHT, tiles_x, tiles_y, slabs))
     diagonal = lax.ppermute(sent, axes, lateral(DIAGONAL, tiles_x, tiles_y, slabs))
@@ -455,6 +461,7 @@
             pltpu.VMEM((depth, LANES), f32),
             pltpu.VMEM((LANES, LANES), f32),
             pltpu.VMEM((rows, cols), jnp.int32),
+            pltpu.VMEM((2, levels, rows, LANES), f32),
             pltpu.SemaphoreType.DMA((1 + 2 * PIECES,)),
         ],
         compiler_params=params,

time: 31.7 us -> 31.4 us (level)
  the two profiles are of different devices: /device:TPU:2 before, /device:TPU:1 now
where the time goes in v3:
time: 31.4 us; the launch traced here: 31.1 us
  starting transfers between devices  7.87 us (25%)
  blocking collectives  7.81 us (25%)
  Pallas kernels  7.75 us (25%)
  waiting for transfers between devices  6.21 us (20%)
  between operations  1.35 us (4%)
    all_to_all x1, blocking collectives, shards(): got = lax.all_to_all(packed, 'gz', 0, 0)  7.81 us
    ppermute x1, waiting for transfers between devices, shards(): lax.ppermute(sent, axes, lateral(STRAIGHT, tiles_x, tiles_y, slabs))  6.21 us
    ppermute x1, starting transfers between devices, shards(): lax.ppermute(sent, axes, lateral(DIAGONAL, tiles_x, tiles_y, slabs))  5.95 us
    pallas_call x1, Pallas kernels, shards(): pl.pallas_call(functools.partial(last_kernel, slabs), out_shape=[jax.Shap...  4.38 us
    pallas_call x1, Pallas kernels, shards(): pl.pallas_call(functools.partial(own_kernel, slabs), out_shape=[jax.Shape...  3.3 us
    ppermute x1, starting transfers between devices, shards(): lax.ppermute(sent, axes, lateral(STRAIGHT, tiles_x, tiles_y, slabs))  1.92 us
  transfers between devices with their start and end apart: 2, of which 1 were waited for; matrix products, arithmetic and copies ran while one was open for 0% of the time, Pallas kernels for 11%

profile of v3, /device:TPU:1, one launch (start us, length us, event | category | flops | bytes accessed | tf_op | source)
XLA Modules:
  0.0 31.1 jit_solution(17592531647355714146)
XLA Ops:
  0.6 0.0 copy-start.1
  1.3 0.0 copy-done.1
  1.3 0.0 copy-start
  1.4 0.1 dynamic_update_slice.3.sent_ref
  1.4 5.9 %collective-permute-start.1 = (f32[40,128]{1,0:T(8,128)S(1)}, f32[40,128]{1,0:T(8,128)S(1)}, u32[]{:S(2)}, u32[]{:S(2)}) collective-permute-start(f32[40,128]{1,0:T(8,128)S(1)} %dynamic_update_slice.3.sent_ref), channel_id=1, source_target_pairs={{133,1},{137,5},{130,6},{141,9},{134,10},{145,13},{138,14},{149,17... | collective-permute-start | bytes 61448 | tf_op jit(solution)/shard_map/ppermute | solution.py:442
  7.4 1.9 %collective-permute-start = (f32[40,128]{1,0:T(8,128)S(1)}, f32[40,128]{1,0:T(8,128)S(1)}, u32[]{:S(2)}, u32[]{:S(2)}) collective-permute-start(f32[40,128]{1,0:T(8,128)S(1)} %dynamic_update_slice.3.sent_ref), channel_id=1, source_target_pairs={{129,1},{7,3},{133,5},{2,6},{11,7},{137,9},{6,10},{15,11},{141,13}... | collective-permute-start | bytes 61448 | tf_op jit(solution)/shard_map/ppermute | solution.py:441
  9.3 0.0 copy-done
  9.3 3.3 %own_tile.1 = (f32[96,128]{1,0:T(8,128)S(1)}, f32[32,128]{1,0:T(8,128)S(1)}, s32[32,128]{1,0:T(8,128)S(1)}, f32[48,32,128]{2,1,0:T(8,128)S(1)}, f32[16,32,96]{2,...) custom-call(f32[16,32,96]{2,1,0:T(8,128)} %u_hbm.1, f32[16,32,96]{2,1,0:T(8,128)} %theta_hbm.1, ...), custom_call_target="tpu_custom_call" | custom-call | flops 2000000000 | bytes 1000000 | tf_op jit(solution)/shard_map/own_tile/pallas_call | solution.py:445
  12.6 0.0 collective-permute-done.1.diagonal_ref
  12.6 6.2 %collective-permute-done.straight_ref = f32[40,128]{1,0:T(8,128)S(1)} collective-permute-done((f32[40,128]{1,0:T(8,128)S(1)}, f32[40,128]{1,0:T(8,128)S(1)}, u32[]{:S(2)}, u32[]{:S(2)}) %collective-permute-start) | collective-permute-done | bytes 20512 | tf_op jit(solution)/shard_map/ppermute | solution.py:441
  18.8 0.1 pack.1
  18.9 7.8 %all_to_all.5.got_ref = f32[4,120,128]{2,1,0:T(8,128)S(1)} all-to-all(f32[4,120,128]{2,1,0:T(8,128)S(1)} %pack.1), channel_id=1, replica_groups=mesh['gx'=8,'gy'=32,'gz'=4] {'gz'}, dimensions={0} | all-to-all | bytes 491520 | tf_op jit(solution)/shard_map/all_to_all | solution.py:477
  26.7 4.4 %solve.1 = (f32[16,32,96]{2,1,0:T(8,128)}, f32[16,32,96]{2,1,0:T(8,128)}) custom-call(f32[4,120,128]{2,1,0:T(8,128)S(1)} %all_to_all.5.got_ref, f32[48,32,128]{2,1,0:T(8,128)S(1)} %get-tuple-element.10.own_ref, f32[16,32,96]{2,1,0:T(8,128)S(1)} %get-tuple-element.11.u_ref, f32[16,32,96]{2,1,0:T(8,128)S(1)} %get-tuple-element.12.theta_ref, ...), custom_call_target="tpu_custom_call" | custom-call | tf_op jit(solution)/shard_map/solve/pallas_call | solution.py:478
  (1 shorter events, 0.0 us)
Async XLA Ops:
  0.6 0.7 %copy-start.1 = (f32[4,1,1,1024]{3,2,1,0:T(1,128)S(1)}, f32[4,1,1,1024]{3,2,1,0:T(1,128)}, u32[]{:S(2)}) copy-start(f32[4,1,1,1024]{3,2,1,0:T(1,128)} %param.8) | copy-start | bytes 49156
  1.3 8.0 %copy-start = (f32[16,64]{1,0:T(8,128)S(1)}, f32[16,64]{1,0:T(8,128)}, u32[]{:S(2)}) copy-start(f32[16,64]{1,0:T(8,128)} %table_ref.1) | copy-start | bytes 12292
  1.4 11.2 %collective-permute-start.1 = (f32[40,128]{1,0:T(8,128)S(1)}, f32[40,128]{1,0:T(8,128)S(1)}, u32[]{:S(2)}, u32[]{:S(2)}) collective-permute-start(f32[40,128]{1,0:T(8,128)S(1)} %dynamic_update_slice.3.sent_ref), channel_id=1, source_target_pairs={{133,1},{137,5},{130,6},{141,9},{134,10},{145,13},{138,14},{149,17... | collective-permute-start | bytes 61448 | tf_op jit(solution)/shard_map/ppermute | solution.py:442
  7.4 11.5 %collective-permute-start = (f32[40,128]{1,0:T(8,128)S(1)}, f32[40,128]{1,0:T(8,128)S(1)}, u32[]{:S(2)}, u32[]{:S(2)}) collective-permute-start(f32[40,128]{1,0:T(8,128)S(1)} %dynamic_update_slice.3.sent_ref), channel_id=1, source_target_pairs={{129,1},{7,3},{133,5},{2,6},{11,7},{137,9},{6,10},{15,11},{141,13}... | collective-permute-start | bytes 61448 | tf_op jit(solution)/shard_map/ppermute | solution.py:441

commit v4 on v3

--- a/solution.py
+++ b/solution.py
@@ -19,7 +19,6 @@
 PIECES = 4
 FINE = HALO // 2
 LOG2E = math.log2(math.e)
-MANY = 8
 ACROSS = (2, 3, 4, 5, 6, 7)
 NT = (((1,), (1,)), ((), ()))
 VMEM_LIMIT = 48 * 1024 * 1024
@@ -50,10 +49,10 @@
     return lax.div(live + (size - 1), size)
 
 
-def in_batches(blocks, add):
+def in_batches(blocks, add, sizes):
     done = jnp.int32(0)
-    for size in (MANY, MANY // 2, MANY // 4):
-        spare = size // 2 - 1 if size > MANY // 4 else size - 1
+    for size in sizes:
+        spare = size // 2 - 1 if size > sizes[-1] else size - 1
         steps = lax.div(blocks - done + spare, size)
 
         def batch(c, carry, done=done, size=size):
@@ -161,7 +160,7 @@
         entries = [(0, first + k, live, 0, 0) for k in range(n)]
         add_points(sent_ref, entries, mix, acc_ref, tuple(range(rows // FINE)), cols)
 
-    in_batches(whole_blocks(live, LANES), add)
+    in_batches(whole_blocks(live, LANES), add, (8, 4, 2))
     copies[0].wait()
     index = widen(klass_ref[...])
     index_ref[...] = index
@@ -379,14 +378,14 @@
             entries = [(number * 32, first + k, live, 0, 0) for k in range(n)]
             add_points(points_ref, entries, mix, acc_ref, steps, cols)
 
-        in_batches(whole_blocks(live, LANES), add)
+        in_batches(whole_blocks(live, LANES), add, (8, 4, 2))
 
     filled = jnp.int32(0)
     for number in ACROSS:
         for k in range(8):
             list_ref[filled + k] = number * 8 + k
         filled = filled + whole_blocks(live_ref[number], LANES)
-    for k in range(MANY):
+    for k in range(8):
         list_ref[filled + k] = SPARE * 8
     side_ref[...] = jnp.zeros_like(side_ref)
     stack_ref[...] = jnp.zeros_like(stack_ref)
@@ -400,7 +399,7 @@
                             at_ref[2 * number + 1]))
         add_sides(points_ref, entries, mix, side_ref, rows, cols)
 
-    in_batches(filled, add_side)
+    in_batches(filled, add_side, (16, 8, 4, 2))
     fields = side_fields(side_ref, index_ref, stack_ref, rows, cols)
     row = lax.broadcasted_iota(jnp.int32, (rows, LANES), 0)
     cross = cross_factor(row // FINE, row % FINE)

time: 31.4 us -> 31.5 us (level)
  the two profiles are of different devices: /device:TPU:1 before, /device:TPU:2 now
where the time goes in v4:
time: 31.5 us; the launch traced here: 30.9 us
  blocking collectives  20.7 us (66%)
  Pallas kernels  6.13 us (19%)
  starting transfers between devices  2.58 us (8%)
  between operations  1.36 us (4%)
    all_to_all x1, blocking collectives, shards(): got = lax.all_to_all(packed, 'gz', 0, 0)  20.7 us
    pallas_call x1, Pallas kernels, shards(): pl.pallas_call(functools.partial(own_kernel, slabs), out_shape=[jax.Shape...  3.3 us
    pallas_call x1, Pallas kernels, shards(): pl.pallas_call(functools.partial(last_kernel, slabs), out_shape=[jax.Shap...  2.76 us
    ppermute x1, starting transfers between devices, shards(): lax.ppermute(sent, axes, lateral(DIAGONAL, tiles_x, tiles_y, slabs))  1.29 us
    ppermute x1, starting transfers between devices, shards(): lax.ppermute(sent, axes, lateral(STRAIGHT, tiles_x, tiles_y, slabs))  1.29 us
  transfers between devices with their start and end apart: 2, of which 0 were waited for; matrix products, arithmetic and copies ran while one was open for 0% of the time, Pallas kernels for 11%

profile of v4, /device:TPU:2, one launch (start us, length us, event | category | flops | bytes accessed | tf_op | source)
XLA Modules:
  0.0 30.9 jit_solution(17100006428969506423)
XLA Ops:
  0.6 0.0 copy-start.1
  1.3 0.0 copy-done.1
  1.3 0.0 copy-start
  1.4 0.1 dynamic_update_slice.3.sent_ref
  1.4 1.3 %collective-permute-start.1 = (f32[40,128]{1,0:T(8,128)S(1)}, f32[40,128]{1,0:T(8,128)S(1)}, u32[]{:S(2)}, u32[]{:S(2)}) collective-permute-start(f32[40,128]{1,0:T(8,128)S(1)} %dynamic_update_slice.3.sent_ref), channel_id=1, source_target_pairs={{133,1},{137,5},{130,6},{141,9},{134,10},{145,13},{138,14},{149,17... | collective-permute-start | bytes 61448 | tf_op jit(solution)/shard_map/ppermute | solution.py:441
  2.7 1.3 %collective-permute-start = (f32[40,128]{1,0:T(8,128)S(1)}, f32[40,128]{1,0:T(8,128)S(1)}, u32[]{:S(2)}, u32[]{:S(2)}) collective-permute-start(f32[40,128]{1,0:T(8,128)S(1)} %dynamic_update_slice.3.sent_ref), channel_id=1, source_target_pairs={{129,1},{7,3},{133,5},{2,6},{11,7},{137,9},{6,10},{15,11},{141,13}... | collective-permute-start | bytes 61448 | tf_op jit(solution)/shard_map/ppermute | solution.py:440
  4.0 0.0 copy-done
  4.0 3.3 %own_tile.1 = (f32[96,128]{1,0:T(8,128)S(1)}, f32[32,128]{1,0:T(8,128)S(1)}, s32[32,128]{1,0:T(8,128)S(1)}, f32[48,32,128]{2,1,0:T(8,128)S(1)}, f32[16,32,96]{2,...) custom-call(f32[16,32,96]{2,1,0:T(8,128)} %u_hbm.1, f32[16,32,96]{2,1,0:T(8,128)} %theta_hbm.1, ...), custom_call_target="tpu_custom_call" | custom-call | flops 2000000000 | bytes 1000000 | tf_op jit(solution)/shard_map/own_tile/pallas_call | solution.py:444
  7.3 0.0 collective-permute-done.1.diagonal_ref
  7.3 0.0 collective-permute-done.straight_ref
  7.4 0.1 pack.1
  7.4 20.7 %all_to_all.5.got_ref = f32[4,120,128]{2,1,0:T(8,128)S(1)} all-to-all(f32[4,120,128]{2,1,0:T(8,128)S(1)} %pack.1), channel_id=1, replica_groups=mesh['gx'=8,'gy'=32,'gz'=4] {'gz'}, dimensions={0} | all-to-all | bytes 491520 | tf_op jit(solution)/shard_map/all_to_all | solution.py:476
  28.1 2.8 %solve.1 = (f32[16,32,96]{2,1,0:T(8,128)}, f32[16,32,96]{2,1,0:T(8,128)}) custom-call(f32[4,120,128]{2,1,0:T(8,128)S(1)} %all_to_all.5.got_ref, f32[48,32,128]{2,1,0:T(8,128)S(1)} %get-tuple-element.10.own_ref, f32[16,32,96]{2,1,0:T(8,128)S(1)} %get-tuple-element.11.u_ref, f32[16,32,96]{2,1,0:T(8,128)S(1)} %get-tuple-element.12.theta_ref, ...), custom_call_target="tpu_custom_call" | custom-call | tf_op jit(solution)/shard_map/solve/pallas_call | solution.py:477
  (1 shorter events, 0.0 us)
Async XLA Ops:
  0.6 0.7 %copy-start.1 = (f32[4,1,1,1024]{3,2,1,0:T(1,128)S(1)}, f32[4,1,1,1024]{3,2,1,0:T(1,128)}, u32[]{:S(2)}) copy-start(f32[4,1,1,1024]{3,2,1,0:T(1,128)} %param.8) | copy-start | bytes 49156
  1.3 2.7 %copy-start = (f32[16,64]{1,0:T(8,128)S(1)}, f32[16,64]{1,0:T(8,128)}, u32[]{:S(2)}) copy-start(f32[16,64]{1,0:T(8,128)} %table_ref.1) | copy-start | bytes 12292
  1.4 5.9 %collective-permute-start.1 = (f32[40,128]{1,0:T(8,128)S(1)}, f32[40,128]{1,0:T(8,128)S(1)}, u32[]{:S(2)}, u32[]{:S(2)}) collective-permute-start(f32[40,128]{1,0:T(8,128)S(1)} %dynamic_update_slice.3.sent_ref), channel_id=1, source_target_pairs={{133,1},{137,5},{130,6},{141,9},{134,10},{145,13},{138,14},{149,17... | collective-permute-start | bytes 61448 | tf_op jit(solution)/shard_map/ppermute | solution.py:441
  2.7 4.6 %collective-permute-start = (f32[40,128]{1,0:T(8,128)S(1)}, f32[40,128]{1,0:T(8,128)S(1)}, u32[]{:S(2)}, u32[]{:S(2)}) collective-permute-start(f32[40,128]{1,0:T(8,128)S(1)} %dynamic_update_slice.3.sent_ref), channel_id=1, source_target_pairs={{129,1},{7,3},{133,5},{2,6},{11,7},{137,9},{6,10},{15,11},{141,13}... | collective-permute-start | bytes 61448 | tf_op jit(solution)/shard_map/ppermute | solution.py:440
